TPU v7x, 256 devices: a whole 4x4x8 slice. The times are simulated.
256 devices in a mesh: segment: 4 (over x), lat: 64 (over z, y, core).
Axes of the slice: x: 4, y: 4, z: 8, core: 2. Of those that a mesh axis runs over, the one named last changes fastest.
Arguments:
- tokens: bfloat16 [4, 4, 768, 6, 512], P(None, None, 'lat'), may hold values from -6 to 6
- norm_gain: float32 [4, 2, 512], P('segment'), may hold values from 0.25 to 1.75
- w_qkv: bfloat16 [4, 512, 1536], P('segment', 'lat'), may hold values from -2 to 2
- w_proj: bfloat16 [4, 512, 512], P('segment', 'lat'), may hold values from -0.25 to 0.25
- w_up: bfloat16 [4, 512, 2048], P('segment', 'lat'), may hold values from -0.25 to 0.25
- w_down: bfloat16 [4, 2048, 512], P('segment', 'lat'), may hold values from -0.125 to 0.125
Outputs:
- block_out: bfloat16 [4, 4, 4, 768, 6, 512], P('segment', None, None, 'lat')
All inputs are finite; a program needn't handle non-finite values.
Results may differ from a plain program's by a relative error of at most 0.017.
Values may be sent and summed in bfloat16 or wider, within the bound.
No kernel may reach another device: no remote copies, remote signals or barrier semaphores. Data moves between devices by JAX's collectives and lax.ppermute only.
A program may use at most 64 MiB of HBM per device.

v0:
```python
import jax
import jax.numpy as jnp
from jax import lax
from jax.sharding import PartitionSpec as P

HEADS = 8
HEAD = 64
LEVELS = 4
LEVWIN = 2
LONWIN = 6


EPS = 1e-05


def padded(cells, sides, width):
    for axis, dim in sides:
        count = lax.axis_size(axis)
        ends = count - 1
        head = lax.slice_in_dim(cells, 0, width, axis=dim)
        tail = lax.slice_in_dim(cells, cells.shape[dim] - width, cells.shape[dim], axis=dim)
        cells = jnp.concatenate(
            [
                lax.ppermute(tail, axis, [(i, (i + 1) % count) for i in range(ends)]),
                cells,
                lax.ppermute(head, axis, [((i + 1) % count, i) for i in range(ends)]),
            ],
            axis=dim,
        )
    return cells


def shifted_2(value, axis, steps):
    count = lax.axis_size(axis)
    first, last = (max(0, -steps), min(count, count - steps))
    return lax.ppermute(value, axis, [(source, source + steps) for source in range(first, last)])


def layer_norm(values, gain):
    wide = values.astype(jnp.float32)
    center = jnp.mean(wide, axis=-1, keepdims=True)
    spread = jnp.mean(jnp.square(wide - center), axis=-1, keepdims=True)
    return (wide - center) * lax.rsqrt(spread + EPS) * gain


def to_windows(field, row_span):
    levels, rows_all, lons, width = field.shape
    shaped = field.reshape(
        levels // LEVWIN, LEVWIN, rows_all // row_span, row_span, lons // LONWIN, LONWIN, width
    )
    shaped = shaped.transpose(0, 2, 4, 1, 3, 5, 6)
    return shaped.reshape(
        levels // LEVWIN, rows_all // row_span, lons // LONWIN, LEVWIN * row_span * LONWIN, width
    )


def from_windows(field, row_span, rows_all, lons):
    width = field.shape[-1]
    shaped = field.reshape(
        LEVELS // LEVWIN, rows_all // row_span, lons // LONWIN, LEVWIN, row_span, LONWIN, width
    )
    shaped = shaped.transpose(0, 3, 1, 4, 2, 5, 6)
    return shaped.reshape(LEVELS, rows_all, lons, width)


def window_mask(query_region, key_region, key_valid, query_span, key_span):
    query_win = to_windows(query_region[..., None], query_span)[..., 0]
    key_win = to_windows(key_region[..., None], key_span)[..., 0]
    valid_win = to_windows(key_valid[..., None], key_span)[..., 0]
    return (query_win[..., :, None] == key_win[..., None, :]) & (valid_win[..., None, :] > 0)


def attend(queries, keys, values, allowed):
    query_heads = queries.reshape(queries.shape[:-1] + (HEADS, HEAD))
    key_heads = keys.reshape(keys.shape[:-1] + (HEADS, HEAD))
    value_heads = values.reshape(values.shape[:-1] + (HEADS, HEAD))
    scores = jnp.einsum(
        "abcqhe,abckhe->abchqk", query_heads, key_heads, preferred_element_type=jnp.float32
    ) * HEAD ** (-0.5)
    scores = jnp.where(allowed[:, :, :, None], scores, -1e30)
    row_top = jnp.max(scores, axis=-1, keepdims=True)
    expo_terms = jnp.exp(scores - row_top)
    probs = (expo_terms / jnp.sum(expo_terms, axis=-1, keepdims=True)).astype(jnp.bfloat16)
    mixed = jnp.einsum(
        "abchqk,abckhe->abcqhe", probs, value_heads, preferred_element_type=jnp.float32
    )
    return mixed.reshape(mixed.shape[:-2] + (HEADS * HEAD,)).astype(jnp.bfloat16)


def swin_block(field, gains, weights, parity, row_place, lat_count):
    proj_qkv, proj_out, proj_up, proj_down = weights
    width = proj_out.shape[0]
    rows_own, lons = (field.shape[1], field.shape[2])
    half_rows = rows_own // 2
    normed = layer_norm(field, gains[0]).astype(jnp.bfloat16)
    packed = jnp.dot(normed, proj_qkv, preferred_element_type=jnp.float32).astype(jnp.bfloat16)
    queries = packed[..., :width]
    keyvals = padded(packed[..., width:], (("lat", 1),), half_rows)
    shifted = parity == 1
    queries = jnp.where(shifted, jnp.roll(queries, -1, 0), queries)
    keyvals = jnp.where(shifted, jnp.roll(keyvals, -1, 0), keyvals)
    region = jnp.where(shifted, jnp.arange(LEVELS) == LEVELS - 1, False).astype(jnp.int32)
    ext_rows = jnp.arange(rows_own + 2 * half_rows, dtype=jnp.int32)
    global_rows = row_place * rows_own - half_rows + ext_rows
    row_valid = ((global_rows >= 0) & (global_rows < rows_own * lat_count)).astype(jnp.int32)
    pieces = []
    for group_index in range(2):
        start = half_rows + (2 * group_index - 1) * half_rows * parity
        group_keys = lax.dynamic_slice_in_dim(keyvals, start, rows_own, 1)
        group_valid = lax.dynamic_slice_in_dim(row_valid, start, rows_own, 0)
        group_queries = queries[:, group_index * half_rows : (group_index + 1) * half_rows]
        query_region = jnp.broadcast_to(region[:, None, None], (LEVELS, half_rows, lons))
        key_region = jnp.broadcast_to(region[:, None, None], (LEVELS, rows_own, lons))
        valid_map = jnp.broadcast_to(group_valid[None, :, None], (LEVELS, rows_own, lons))
        allowed = window_mask(query_region, key_region, valid_map, half_rows, rows_own)
        key_win = to_windows(group_keys, rows_own)
        mixed = attend(
            to_windows(group_queries, half_rows),
            key_win[..., :width],
            key_win[..., width:],
            allowed,
        )
        pieces.append(from_windows(mixed, half_rows, half_rows, lons))
    mixed = jnp.concatenate(pieces, axis=1)
    mixed = jnp.where(shifted, jnp.roll(mixed, 1, 0), mixed)
    residual = field.astype(jnp.float32) + jnp.dot(
        mixed, proj_out, preferred_element_type=jnp.float32
    )
    inner_norm = layer_norm(residual, gains[1]).astype(jnp.bfloat16)
    hidden = jax.nn.gelu(jnp.dot(inner_norm, proj_up, preferred_element_type=jnp.float32)).astype(
        jnp.bfloat16
    )
    return (residual + jnp.dot(hidden, proj_down, preferred_element_type=jnp.float32)).astype(
        jnp.bfloat16
    )


def on_device(tokens, norm_gain, w_qkv, w_proj, w_up, w_down):
    segment_index = lax.axis_index("segment")
    last_segment = lax.axis_size("segment") - 1
    parity = segment_index % 2
    row_place = lax.axis_index("lat")
    lat_count = lax.axis_size("lat")
    weights = (
        lax.all_gather(w_qkv[0], "lat", axis=0, tiled=True),
        lax.all_gather(w_proj[0], "lat", axis=0, tiled=True),
        lax.all_gather(w_up[0], "lat", axis=0, tiled=True),
        lax.all_gather(w_down[0], "lat", axis=0, tiled=True),
    )
    gains = norm_gain[0]
    micro_count = tokens.shape[0]
    blank = jnp.zeros(tokens.shape, jnp.bfloat16)

    def tick(tick_step, carry):
        outputs, skip_store, incoming = carry
        entry_slot = jnp.minimum(tick_step, micro_count - 1)
        entering = lax.dynamic_index_in_dim(tokens, entry_slot, 0, keepdims=False)
        work_slot = jnp.clip(tick_step - segment_index, 0, micro_count - 1)
        stored_skip = lax.dynamic_index_in_dim(skip_store, work_slot, 0, keepdims=False)
        joined = (incoming.astype(jnp.float32) + stored_skip.astype(jnp.float32)).astype(
            jnp.bfloat16
        )
        source = jnp.where(
            segment_index == 0, entering, jnp.where(segment_index == last_segment, joined, incoming)
        )
        result = swin_block(source, gains, weights, parity, row_place, lat_count)
        active = (tick_step >= segment_index) & (tick_step - segment_index < micro_count)
        previous = lax.dynamic_index_in_dim(outputs, work_slot, 0, keepdims=False)
        outputs = lax.dynamic_update_index_in_dim(
            outputs, jnp.where(active, result, previous), work_slot, 0
        )
        incoming = shifted_2(result, "segment", 1)
        arrived = shifted_2(result, "segment", 3)
        older = lax.dynamic_index_in_dim(skip_store, entry_slot, 0, keepdims=False)
        keep_new = (segment_index == last_segment) & (tick_step < micro_count)
        skip_store = lax.dynamic_update_index_in_dim(
            skip_store, jnp.where(keep_new, arrived, older), entry_slot, 0
        )
        return (outputs, skip_store, incoming)

    outputs, skip_store, incoming = lax.fori_loop(
        0, micro_count + 3, tick, (blank, blank, blank[0])
    )
    return outputs[None]


def solution(mesh):
    return jax.shard_map(
        on_device,
        mesh=mesh,
        in_specs=(
            P(None, None, "lat", None, None),
            P("segment", None, None),
            P("segment", "lat", None),
            P("segment", "lat", None),
            P("segment", "lat", None),
            P("segment", "lat", None),
        ),
        out_specs=P("segment", None, None, "lat", None, None),
        check_vma=False,
    )
```

profile of v0, /device:TPU:134, one launch (start us, length us, event | category | flops | bytes accessed | tf_op | source)
XLA Modules:
  0.0 674.8 jit_solution(4194854052836120334)
XLA Ops:
  8.8 54.4 %all-gather.1 = bf16[1,512,512]{2,1,0:T(8,128)(2,1)} all-gather(bf16[1,8,512]{2,1,0:T(8,128)(2,1)} %param.11), channel_id=3, replica_groups=mesh['segment'=4,'lat'=64] {'lat'}, dimensions={1}, use_global_device_ids=true | all-gather | bytes 532480 | tf_op jit(solution)/shard_map/all_gather | solution.py:146
  63.2 22.8 %all-gather.8.cloned.1.call-done = bf16[1,512,1536]{2,1,0:T(8,128)(2,1)} async-done(((bf16[1,8,1536]{2,1,0:T(8,128)(2,1)}), bf16[1,512,1536]{2,1,0:T(8,128)(2,1)}) %all-gather.8.cloned.1.call-update) | async-done | bytes 1572880 | tf_op jit(solution)/shard_map/all_gather | solution.py:145
  86.0 77.7 %all-gather.10.cloned.1.call-done = bf16[1,512,2048]{2,1,0:T(8,128)(2,1)} async-done(((bf16[1,8,2048]{2,1,0:T(8,128)(2,1)}), bf16[1,512,2048]{2,1,0:T(8,128)(2,1)}) %all-gather.10.cloned.1.call-update) | async-done | bytes 2097168 | tf_op jit(solution)/shard_map/all_gather | solution.py:147
  163.8 77.8 %all-gather.12.cloned.1.call-done = bf16[1,2048,512]{2,1,0:T(8,128)(2,1)} async-done(((bf16[1,32,512]{2,1,0:T(8,128)(2,1)}), bf16[1,2048,512]{2,1,0:T(8,128)(2,1)}) %all-gather.12.cloned.1.call-update) | async-done | bytes 2097168 | tf_op jit(solution)/shard_map/all_gather | solution.py:148
  245.0 423.3 %while.20 = (s32[]{:T(128)}, bf16[4,4,12,6,512]{4,1,3,2,0:T(4,128)(2,1)}, bf16[4,4,12,6,512]{4,3,2,1,0:T(8,128)(2,1)}, bf16[4,12,6,512]{3,2,1,0:T(8,128)(2,1)}, ...) while((s32[]{:T(128)}, ...), condition=%wide.region_9.10_spmd, body=%wide.region_0.9_spmd.sunk | while | flops 1956991232 | bytes 57775784 | solution.py:181
  248.0 2.3 convolution_convert_fusion.4
  251.3 5.4 collective-permute-start
  267.0 2.3 collective-permute-done.1
  277.2 2.4 fusion.145
  284.1 3.7 fusion.146
  289.7 5.2 fusion.152
  298.6 7.2 %collective-permute-done.2 = bf16[4,12,6,512]{3,2,1,0:T(8,128)(2,1)S(1)} collective-permute-done((bf16[4,12,6,512]{3,2,1,0:T(8,128)(2,1)S(1)}, bf16[4,12,6,512]{3,2,1,0:T(8,128)(2,1)S(1)}, u32[]{:S(2)}, u32[]{:S(2)}) %collective-permute-start.2) | collective-permute-done | bytes 294944 | tf_op jit(solution)/shard_map/while/body/eval_jaxpr/ppermute | solution.py:36
  312.9 4.1 collective-permute-start
  327.3 2.3 collective-permute-done.1
  337.6 2.4 fusion.145
  344.4 3.7 fusion.146
  350.1 5.2 fusion.152
  358.9 7.2 %collective-permute-done.2 = bf16[4,12,6,512]{3,2,1,0:T(8,128)(2,1)S(1)} collective-permute-done((bf16[4,12,6,512]{3,2,1,0:T(8,128)(2,1)S(1)}, bf16[4,12,6,512]{3,2,1,0:T(8,128)(2,1)S(1)}, u32[]{:S(2)}, u32[]{:S(2)}) %collective-permute-start.2) | collective-permute-done | bytes 294944 | tf_op jit(solution)/shard_map/while/body/eval_jaxpr/ppermute | solution.py:36
  373.3 3.9 collective-permute-start
  387.5 2.3 collective-permute-done.1
  397.7 2.4 fusion.145
  404.5 3.7 fusion.146
  410.2 5.2 fusion.152
  419.0 7.2 %collective-permute-done.2 = bf16[4,12,6,512]{3,2,1,0:T(8,128)(2,1)S(1)} collective-permute-done((bf16[4,12,6,512]{3,2,1,0:T(8,128)(2,1)S(1)}, bf16[4,12,6,512]{3,2,1,0:T(8,128)(2,1)S(1)}, u32[]{:S(2)}, u32[]{:S(2)}) %collective-permute-start.2) | collective-permute-done | bytes 294944 | tf_op jit(solution)/shard_map/while/body/eval_jaxpr/ppermute | solution.py:36
  433.4 4.0 collective-permute-start
  447.8 2.3 collective-permute-done.1
  458.0 2.4 fusion.145
  464.9 3.7 fusion.146
  470.5 5.2 fusion.152
  479.4 7.2 %collective-permute-done.2 = bf16[4,12,6,512]{3,2,1,0:T(8,128)(2,1)S(1)} collective-permute-done((bf16[4,12,6,512]{3,2,1,0:T(8,128)(2,1)S(1)}, bf16[4,12,6,512]{3,2,1,0:T(8,128)(2,1)S(1)}, u32[]{:S(2)}, u32[]{:S(2)}) %collective-permute-start.2) | collective-permute-done | bytes 294944 | tf_op jit(solution)/shard_map/while/body/eval_jaxpr/ppermute | solution.py:36
  493.7 4.0 collective-permute-start
  508.1 2.3 collective-permute-done.1
  518.3 2.4 fusion.145
  525.1 3.7 fusion.146
  530.8 5.2 fusion.152
  539.6 7.2 %collective-permute-done.2 = bf16[4,12,6,512]{3,2,1,0:T(8,128)(2,1)S(1)} collective-permute-done((bf16[4,12,6,512]{3,2,1,0:T(8,128)(2,1)S(1)}, bf16[4,12,6,512]{3,2,1,0:T(8,128)(2,1)S(1)}, u32[]{:S(2)}, u32[]{:S(2)}) %collective-permute-start.2) | collective-permute-done | bytes 294944 | tf_op jit(solution)/shard_map/while/body/eval_jaxpr/ppermute | solution.py:36
  554.0 4.0 collective-permute-start
  568.3 2.3 collective-permute-done.1
  578.6 2.4 fusion.145
  585.4 3.7 fusion.146
  591.0 5.2 fusion.152
  599.9 7.2 %collective-permute-done.2 = bf16[4,12,6,512]{3,2,1,0:T(8,128)(2,1)S(1)} collective-permute-done((bf16[4,12,6,512]{3,2,1,0:T(8,128)(2,1)S(1)}, bf16[4,12,6,512]{3,2,1,0:T(8,128)(2,1)S(1)}, u32[]{:S(2)}, u32[]{:S(2)}) %collective-permute-start.2) | collective-permute-done | bytes 294944 | tf_op jit(solution)/shard_map/while/body/eval_jaxpr/ppermute | solution.py:36
  614.3 4.0 collective-permute-start
  628.6 2.3 collective-permute-done.1
  638.8 2.4 fusion.145
  645.7 3.7 fusion.146
  651.3 5.2 fusion.152
  660.2 7.2 %collective-permute-done.2 = bf16[4,12,6,512]{3,2,1,0:T(8,128)(2,1)S(1)} collective-permute-done((bf16[4,12,6,512]{3,2,1,0:T(8,128)(2,1)S(1)}, bf16[4,12,6,512]{3,2,1,0:T(8,128)(2,1)S(1)}, u32[]{:S(2)}, u32[]{:S(2)}) %collective-permute-start.2) | collective-permute-done | bytes 294944 | tf_op jit(solution)/shard_map/while/body/eval_jaxpr/ppermute | solution.py:36
  (542 shorter events, 248.8 us)
Async XLA Ops:
  6.5 79.5 %all-gather.8.cloned.1.call-start = ((), (), s32[]{:S(2)}) async-start(), calls=%async_computation | async-start | bytes 1597440 | tf_op jit(solution)/shard_map/all_gather | solution.py:145
  7.3 156.5 %all-gather.10.cloned.1.call-start = ((), (), s32[]{:S(2)}) async-start(), calls=%async_computation.1 | async-start | bytes 2129920 | tf_op jit(solution)/shard_map/all_gather | solution.py:147
  8.0 233.5 %all-gather.12.cloned.1.call-start = ((), (), s32[]{:S(2)}) async-start(), calls=%async_computation.2 | async-start | bytes 2129920 | tf_op jit(solution)/shard_map/all_gather | solution.py:148
  242.9 2.1 copy-start.5
  251.3 15.7 %collective-permute-start = (bf16[4,6,6,1024]{3,2,1,0:T(8,128)(2,1)}, bf16[4,6,6,1024]{3,2,1,0:T(8,128)(2,1)S(1)}, u32[]{:S(2)}, u32[]{:S(2)}) collective-permute-start(bf16[4,6,6,1024]{3,2,1,0:T(8,128)(2,1)} %get-tuple-element.614), channel_id=1, source_target_pairs={{1,0},{2,1},{3,2},{4,3},{5,4},{6,5},{7,6},{8,7},{9,8},{10,9},{11,1... | collective-permute-start | bytes 884744 | tf_op jit(solution)/shard_map/while/body/eval_jaxpr/ppermute | solution.py:26
  256.7 12.6 %collective-permute-start.1 = (bf16[4,6,6,1024]{3,2,1,0:T(8,128)(2,1)}, bf16[4,6,6,1024]{3,2,1,0:T(8,128)(2,1)S(1)}, u32[]{:S(2)}, u32[]{:S(2)}) collective-permute-start(bf16[4,6,6,1024]{3,2,1,0:T(8,128)(2,1)} %get-tuple-element.615), channel_id=1, source_target_pairs={{0,1},{1,2},{2,3},{3,4},{4,5},{5,6},{6,7},{7,8},{8,9},{9,10},{10,1... | collective-permute-start | bytes 884744 | tf_op jit(solution)/shard_map/while/body/eval_jaxpr/ppermute | solution.py:24
  277.2 2.4 copy-start.3
  287.8 1.0 copy-start.4
  289.7 7.8 %copy-start.2 = (bf16[1,4,12,6,512]{4,1,3,2,0:T(4,128)(2,1)S(1)}, bf16[1,4,12,6,512]{4,1,3,2,0:T(4,128)(2,1)}, u32[]{:S(2)}) copy-start(bf16[1,4,12,6,512]{4,1,3,2,0:T(4,128)(2,1)} %constant_dynamic-slice_fusion.11) | copy-start | bytes 884740 | tf_op jit(solution)/shard_map/while
  294.9 10.9 %collective-permute-start.2 = (bf16[4,12,6,512]{3,2,1,0:T(8,128)(2,1)S(1)}, bf16[4,12,6,512]{3,2,1,0:T(8,128)(2,1)S(1)}, u32[]{:S(2)}, u32[]{:S(2)}) collective-permute-start(bf16[4,12,6,512]{3,2,1,0:T(8,128)(2,1)S(1)} %fusion.152), channel_id=1, source_target_pairs={{0,192},{1,193},{2,194},{3,195},{4,196},{5,197},{6,198},{7,199},{8... | collective-permute-start | bytes 884744 | tf_op jit(solution)/shard_map/while/body/eval_jaxpr/ppermute | solution.py:36
  296.2 10.4 %collective-permute-start.3 = (bf16[4,12,6,512]{3,2,1,0:T(8,128)(2,1)S(1)}, bf16[4,12,6,512]{3,2,1,0:T(8,128)(2,1)}, u32[]{:S(2)}, u32[]{:S(2)}) collective-permute-start(bf16[4,12,6,512]{3,2,1,0:T(8,128)(2,1)S(1)} %fusion.152), channel_id=1, source_target_pairs={{0,64},{64,128},{128,192},{1,65},{65,129},{129,193},{2,66},{66,130... | collective-permute-start | bytes 884744 | tf_op jit(solution)/shard_map/while/body/eval_jaxpr/ppermute | solution.py:36
  312.9 14.4 %collective-permute-start = (bf16[4,6,6,1024]{3,2,1,0:T(8,128)(2,1)}, bf16[4,6,6,1024]{3,2,1,0:T(8,128)(2,1)S(1)}, u32[]{:S(2)}, u32[]{:S(2)}) collective-permute-start(bf16[4,6,6,1024]{3,2,1,0:T(8,128)(2,1)} %get-tuple-element.614), channel_id=1, source_target_pairs={{1,0},{2,1},{3,2},{4,3},{5,4},{6,5},{7,6},{8,7},{9,8},{10,9},{11,1... | collective-permute-start | bytes 884744 | tf_op jit(solution)/shard_map/while/body/eval_jaxpr/ppermute | solution.py:26
  317.0 12.6 %collective-permute-start.1 = (bf16[4,6,6,1024]{3,2,1,0:T(8,128)(2,1)}, bf16[4,6,6,1024]{3,2,1,0:T(8,128)(2,1)S(1)}, u32[]{:S(2)}, u32[]{:S(2)}) collective-permute-start(bf16[4,6,6,1024]{3,2,1,0:T(8,128)(2,1)} %get-tuple-element.615), channel_id=1, source_target_pairs={{0,1},{1,2},{2,3},{3,4},{4,5},{5,6},{6,7},{7,8},{8,9},{9,10},{10,1... | collective-permute-start | bytes 884744 | tf_op jit(solution)/shard_map/while/body/eval_jaxpr/ppermute | solution.py:24
  337.6 2.4 copy-start.3
  350.1 7.8 %copy-start.2 = (bf16[1,4,12,6,512]{4,1,3,2,0:T(4,128)(2,1)S(1)}, bf16[1,4,12,6,512]{4,1,3,2,0:T(4,128)(2,1)}, u32[]{:S(2)}) copy-start(bf16[1,4,12,6,512]{4,1,3,2,0:T(4,128)(2,1)} %constant_dynamic-slice_fusion.11) | copy-start | bytes 884740 | tf_op jit(solution)/shard_map/while
  355.3 10.9 %collective-permute-start.2 = (bf16[4,12,6,512]{3,2,1,0:T(8,128)(2,1)S(1)}, bf16[4,12,6,512]{3,2,1,0:T(8,128)(2,1)S(1)}, u32[]{:S(2)}, u32[]{:S(2)}) collective-permute-start(bf16[4,12,6,512]{3,2,1,0:T(8,128)(2,1)S(1)} %fusion.152), channel_id=1, source_target_pairs={{0,192},{1,193},{2,194},{3,195},{4,196},{5,197},{6,198},{7,199},{8... | collective-permute-start | bytes 884744 | tf_op jit(solution)/shard_map/while/body/eval_jaxpr/ppermute | solution.py:36
  356.6 10.4 %collective-permute-start.3 = (bf16[4,12,6,512]{3,2,1,0:T(8,128)(2,1)S(1)}, bf16[4,12,6,512]{3,2,1,0:T(8,128)(2,1)}, u32[]{:S(2)}, u32[]{:S(2)}) collective-permute-start(bf16[4,12,6,512]{3,2,1,0:T(8,128)(2,1)S(1)} %fusion.152), channel_id=1, source_target_pairs={{0,64},{64,128},{128,192},{1,65},{65,129},{129,193},{2,66},{66,130... | collective-permute-start | bytes 884744 | tf_op jit(solution)/shard_map/while/body/eval_jaxpr/ppermute | solution.py:36
  373.3 14.2 %collective-permute-start = (bf16[4,6,6,1024]{3,2,1,0:T(8,128)(2,1)}, bf16[4,6,6,1024]{3,2,1,0:T(8,128)(2,1)S(1)}, u32[]{:S(2)}, u32[]{:S(2)}) collective-permute-start(bf16[4,6,6,1024]{3,2,1,0:T(8,128)(2,1)} %get-tuple-element.614), channel_id=1, source_target_pairs={{1,0},{2,1},{3,2},{4,3},{5,4},{6,5},{7,6},{8,7},{9,8},{10,9},{11,1... | collective-permute-start | bytes 884744 | tf_op jit(solution)/shard_map/while/body/eval_jaxpr/ppermute | solution.py:26
  377.2 12.6 %collective-permute-start.1 = (bf16[4,6,6,1024]{3,2,1,0:T(8,128)(2,1)}, bf16[4,6,6,1024]{3,2,1,0:T(8,128)(2,1)S(1)}, u32[]{:S(2)}, u32[]{:S(2)}) collective-permute-start(bf16[4,6,6,1024]{3,2,1,0:T(8,128)(2,1)} %get-tuple-element.615), channel_id=1, source_target_pairs={{0,1},{1,2},{2,3},{3,4},{4,5},{5,6},{6,7},{7,8},{8,9},{9,10},{10,1... | collective-permute-start | bytes 884744 | tf_op jit(solution)/shard_map/while/body/eval_jaxpr/ppermute | solution.py:24
  397.7 2.4 copy-start.3
  408.3 1.0 copy-start.4
  410.2 7.8 %copy-start.2 = (bf16[1,4,12,6,512]{4,1,3,2,0:T(4,128)(2,1)S(1)}, bf16[1,4,12,6,512]{4,1,3,2,0:T(4,128)(2,1)}, u32[]{:S(2)}) copy-start(bf16[1,4,12,6,512]{4,1,3,2,0:T(4,128)(2,1)} %constant_dynamic-slice_fusion.11) | copy-start | bytes 884740 | tf_op jit(solution)/shard_map/while
  415.4 10.9 %collective-permute-start.2 = (bf16[4,12,6,512]{3,2,1,0:T(8,128)(2,1)S(1)}, bf16[4,12,6,512]{3,2,1,0:T(8,128)(2,1)S(1)}, u32[]{:S(2)}, u32[]{:S(2)}) collective-permute-start(bf16[4,12,6,512]{3,2,1,0:T(8,128)(2,1)S(1)} %fusion.152), channel_id=1, source_target_pairs={{0,192},{1,193},{2,194},{3,195},{4,196},{5,197},{6,198},{7,199},{8... | collective-permute-start | bytes 884744 | tf_op jit(solution)/shard_map/while/body/eval_jaxpr/ppermute | solution.py:36
  416.7 10.5 %collective-permute-start.3 = (bf16[4,12,6,512]{3,2,1,0:T(8,128)(2,1)S(1)}, bf16[4,12,6,512]{3,2,1,0:T(8,128)(2,1)}, u32[]{:S(2)}, u32[]{:S(2)}) collective-permute-start(bf16[4,12,6,512]{3,2,1,0:T(8,128)(2,1)S(1)} %fusion.152), channel_id=1, source_target_pairs={{0,64},{64,128},{128,192},{1,65},{65,129},{129,193},{2,66},{66,130... | collective-permute-start | bytes 884744 | tf_op jit(solution)/shard_map/while/body/eval_jaxpr/ppermute | solution.py:36
  433.4 14.4 %collective-permute-start = (bf16[4,6,6,1024]{3,2,1,0:T(8,128)(2,1)}, bf16[4,6,6,1024]{3,2,1,0:T(8,128)(2,1)S(1)}, u32[]{:S(2)}, u32[]{:S(2)}) collective-permute-start(bf16[4,6,6,1024]{3,2,1,0:T(8,128)(2,1)} %get-tuple-element.614), channel_id=1, source_target_pairs={{1,0},{2,1},{3,2},{4,3},{5,4},{6,5},{7,6},{8,7},{9,8},{10,9},{11,1... | collective-permute-start | bytes 884744 | tf_op jit(solution)/shard_map/while/body/eval_jaxpr/ppermute | solution.py:26
  437.5 12.6 %collective-permute-start.1 = (bf16[4,6,6,1024]{3,2,1,0:T(8,128)(2,1)}, bf16[4,6,6,1024]{3,2,1,0:T(8,128)(2,1)S(1)}, u32[]{:S(2)}, u32[]{:S(2)}) collective-permute-start(bf16[4,6,6,1024]{3,2,1,0:T(8,128)(2,1)} %get-tuple-element.615), channel_id=1, source_target_pairs={{0,1},{1,2},{2,3},{3,4},{4,5},{5,6},{6,7},{7,8},{8,9},{9,10},{10,1... | collective-permute-start | bytes 884744 | tf_op jit(solution)/shard_map/while/body/eval_jaxpr/ppermute | solution.py:24
  458.0 2.4 copy-start.3
  470.5 7.8 %copy-start.2 = (bf16[1,4,12,6,512]{4,1,3,2,0:T(4,128)(2,1)S(1)}, bf16[1,4,12,6,512]{4,1,3,2,0:T(4,128)(2,1)}, u32[]{:S(2)}) copy-start(bf16[1,4,12,6,512]{4,1,3,2,0:T(4,128)(2,1)} %constant_dynamic-slice_fusion.11) | copy-start | bytes 884740 | tf_op jit(solution)/shard_map/while
  475.7 10.9 %collective-permute-start.2 = (bf16[4,12,6,512]{3,2,1,0:T(8,128)(2,1)S(1)}, bf16[4,12,6,512]{3,2,1,0:T(8,128)(2,1)S(1)}, u32[]{:S(2)}, u32[]{:S(2)}) collective-permute-start(bf16[4,12,6,512]{3,2,1,0:T(8,128)(2,1)S(1)} %fusion.152), channel_id=1, source_target_pairs={{0,192},{1,193},{2,194},{3,195},{4,196},{5,197},{6,198},{7,199},{8... | collective-permute-start | bytes 884744 | tf_op jit(solution)/shard_map/while/body/eval_jaxpr/ppermute | solution.py:36
  477.0 10.5 %collective-permute-start.3 = (bf16[4,12,6,512]{3,2,1,0:T(8,128)(2,1)S(1)}, bf16[4,12,6,512]{3,2,1,0:T(8,128)(2,1)}, u32[]{:S(2)}, u32[]{:S(2)}) collective-permute-start(bf16[4,12,6,512]{3,2,1,0:T(8,128)(2,1)S(1)} %fusion.152), channel_id=1, source_target_pairs={{0,64},{64,128},{128,192},{1,65},{65,129},{129,193},{2,66},{66,130... | collective-permute-start | bytes 884744 | tf_op jit(solution)/shard_map/while/body/eval_jaxpr/ppermute | solution.py:36
  493.7 14.3 %collective-permute-start = (bf16[4,6,6,1024]{3,2,1,0:T(8,128)(2,1)}, bf16[4,6,6,1024]{3,2,1,0:T(8,128)(2,1)S(1)}, u32[]{:S(2)}, u32[]{:S(2)}) collective-permute-start(bf16[4,6,6,1024]{3,2,1,0:T(8,128)(2,1)} %get-tuple-element.614), channel_id=1, source_target_pairs={{1,0},{2,1},{3,2},{4,3},{5,4},{6,5},{7,6},{8,7},{9,8},{10,9},{11,1... | collective-permute-start | bytes 884744 | tf_op jit(solution)/shard_map/while/body/eval_jaxpr/ppermute | solution.py:26
  497.7 12.6 %collective-permute-start.1 = (bf16[4,6,6,1024]{3,2,1,0:T(8,128)(2,1)}, bf16[4,6,6,1024]{3,2,1,0:T(8,128)(2,1)S(1)}, u32[]{:S(2)}, u32[]{:S(2)}) collective-permute-start(bf16[4,6,6,1024]{3,2,1,0:T(8,128)(2,1)} %get-tuple-element.615), channel_id=1, source_target_pairs={{0,1},{1,2},{2,3},{3,4},{4,5},{5,6},{6,7},{7,8},{8,9},{9,10},{10,1... | collective-permute-start | bytes 884744 | tf_op jit(solution)/shard_map/while/body/eval_jaxpr/ppermute | solution.py:24
  518.3 2.4 copy-start.3
  530.8 7.8 %copy-start.2 = (bf16[1,4,12,6,512]{4,1,3,2,0:T(4,128)(2,1)S(1)}, bf16[1,4,12,6,512]{4,1,3,2,0:T(4,128)(2,1)}, u32[]{:S(2)}) copy-start(bf16[1,4,12,6,512]{4,1,3,2,0:T(4,128)(2,1)} %constant_dynamic-slice_fusion.11) | copy-start | bytes 884740 | tf_op jit(solution)/shard_map/while
  536.0 10.9 %collective-permute-start.2 = (bf16[4,12,6,512]{3,2,1,0:T(8,128)(2,1)S(1)}, bf16[4,12,6,512]{3,2,1,0:T(8,128)(2,1)S(1)}, u32[]{:S(2)}, u32[]{:S(2)}) collective-permute-start(bf16[4,12,6,512]{3,2,1,0:T(8,128)(2,1)S(1)} %fusion.152), channel_id=1, source_target_pairs={{0,192},{1,193},{2,194},{3,195},{4,196},{5,197},{6,198},{7,199},{8... | collective-permute-start | bytes 884744 | tf_op jit(solution)/shard_map/while/body/eval_jaxpr/ppermute | solution.py:36
  537.3 10.5 %collective-permute-start.3 = (bf16[4,12,6,512]{3,2,1,0:T(8,128)(2,1)S(1)}, bf16[4,12,6,512]{3,2,1,0:T(8,128)(2,1)}, u32[]{:S(2)}, u32[]{:S(2)}) collective-permute-start(bf16[4,12,6,512]{3,2,1,0:T(8,128)(2,1)S(1)} %fusion.152), channel_id=1, source_target_pairs={{0,64},{64,128},{128,192},{1,65},{65,129},{129,193},{2,66},{66,130... | collective-permute-start | bytes 884744 | tf_op jit(solution)/shard_map/while/body/eval_jaxpr/ppermute | solution.py:36
  554.0 14.3 %collective-permute-start = (bf16[4,6,6,1024]{3,2,1,0:T(8,128)(2,1)}, bf16[4,6,6,1024]{3,2,1,0:T(8,128)(2,1)S(1)}, u32[]{:S(2)}, u32[]{:S(2)}) collective-permute-start(bf16[4,6,6,1024]{3,2,1,0:T(8,128)(2,1)} %get-tuple-element.614), channel_id=1, source_target_pairs={{1,0},{2,1},{3,2},{4,3},{5,4},{6,5},{7,6},{8,7},{9,8},{10,9},{11,1... | collective-permute-start | bytes 884744 | tf_op jit(solution)/shard_map/while/body/eval_jaxpr/ppermute | solution.py:26
  558.0 12.6 %collective-permute-start.1 = (bf16[4,6,6,1024]{3,2,1,0:T(8,128)(2,1)}, bf16[4,6,6,1024]{3,2,1,0:T(8,128)(2,1)S(1)}, u32[]{:S(2)}, u32[]{:S(2)}) collective-permute-start(bf16[4,6,6,1024]{3,2,1,0:T(8,128)(2,1)} %get-tuple-element.615), channel_id=1, source_target_pairs={{0,1},{1,2},{2,3},{3,4},{4,5},{5,6},{6,7},{7,8},{8,9},{9,10},{10,1... | collective-permute-start | bytes 884744 | tf_op jit(solution)/shard_map/while/body/eval_jaxpr/ppermute | solution.py:24
  578.6 2.4 copy-start.3
  591.0 7.8 %copy-start.2 = (bf16[1,4,12,6,512]{4,1,3,2,0:T(4,128)(2,1)S(1)}, bf16[1,4,12,6,512]{4,1,3,2,0:T(4,128)(2,1)}, u32[]{:S(2)}) copy-start(bf16[1,4,12,6,512]{4,1,3,2,0:T(4,128)(2,1)} %constant_dynamic-slice_fusion.11) | copy-start | bytes 884740 | tf_op jit(solution)/shard_map/while
  596.3 10.9 %collective-permute-start.2 = (bf16[4,12,6,512]{3,2,1,0:T(8,128)(2,1)S(1)}, bf16[4,12,6,512]{3,2,1,0:T(8,128)(2,1)S(1)}, u32[]{:S(2)}, u32[]{:S(2)}) collective-permute-start(bf16[4,12,6,512]{3,2,1,0:T(8,128)(2,1)S(1)} %fusion.152), channel_id=1, source_target_pairs={{0,192},{1,193},{2,194},{3,195},{4,196},{5,197},{6,198},{7,199},{8... | collective-permute-start | bytes 884744 | tf_op jit(solution)/shard_map/while/body/eval_jaxpr/ppermute | solution.py:36
  597.6 10.5 %collective-permute-start.3 = (bf16[4,12,6,512]{3,2,1,0:T(8,128)(2,1)S(1)}, bf16[4,12,6,512]{3,2,1,0:T(8,128)(2,1)}, u32[]{:S(2)}, u32[]{:S(2)}) collective-permute-start(bf16[4,12,6,512]{3,2,1,0:T(8,128)(2,1)S(1)} %fusion.152), channel_id=1, source_target_pairs={{0,64},{64,128},{128,192},{1,65},{65,129},{129,193},{2,66},{66,130... | collective-permute-start | bytes 884744 | tf_op jit(solution)/shard_map/while/body/eval_jaxpr/ppermute | solution.py:36
  614.3 14.3 %collective-permute-start = (bf16[4,6,6,1024]{3,2,1,0:T(8,128)(2,1)}, bf16[4,6,6,1024]{3,2,1,0:T(8,128)(2,1)S(1)}, u32[]{:S(2)}, u32[]{:S(2)}) collective-permute-start(bf16[4,6,6,1024]{3,2,1,0:T(8,128)(2,1)} %get-tuple-element.614), channel_id=1, source_target_pairs={{1,0},{2,1},{3,2},{4,3},{5,4},{6,5},{7,6},{8,7},{9,8},{10,9},{11,1... | collective-permute-start | bytes 884744 | tf_op jit(solution)/shard_map/while/body/eval_jaxpr/ppermute | solution.py:26
  618.3 12.6 %collective-permute-start.1 = (bf16[4,6,6,1024]{3,2,1,0:T(8,128)(2,1)}, bf16[4,6,6,1024]{3,2,1,0:T(8,128)(2,1)S(1)}, u32[]{:S(2)}, u32[]{:S(2)}) collective-permute-start(bf16[4,6,6,1024]{3,2,1,0:T(8,128)(2,1)} %get-tuple-element.615), channel_id=1, source_target_pairs={{0,1},{1,2},{2,3},{3,4},{4,5},{5,6},{6,7},{7,8},{8,9},{9,10},{10,1... | collective-permute-start | bytes 884744 | tf_op jit(solution)/shard_map/while/body/eval_jaxpr/ppermute | solution.py:24
  638.8 2.4 copy-start.3
  651.3 7.8 %copy-start.2 = (bf16[1,4,12,6,512]{4,1,3,2,0:T(4,128)(2,1)S(1)}, bf16[1,4,12,6,512]{4,1,3,2,0:T(4,128)(2,1)}, u32[]{:S(2)}) copy-start(bf16[1,4,12,6,512]{4,1,3,2,0:T(4,128)(2,1)} %constant_dynamic-slice_fusion.11) | copy-start | bytes 884740 | tf_op jit(solution)/shard_map/while
  656.5 10.9 %collective-permute-start.2 = (bf16[4,12,6,512]{3,2,1,0:T(8,128)(2,1)S(1)}, bf16[4,12,6,512]{3,2,1,0:T(8,128)(2,1)S(1)}, u32[]{:S(2)}, u32[]{:S(2)}) collective-permute-start(bf16[4,12,6,512]{3,2,1,0:T(8,128)(2,1)S(1)} %fusion.152), channel_id=1, source_target_pairs={{0,192},{1,193},{2,194},{3,195},{4,196},{5,197},{6,198},{7,199},{8... | collective-permute-start | bytes 884744 | tf_op jit(solution)/shard_map/while/body/eval_jaxpr/ppermute | solution.py:36
  657.8 10.5 %collective-permute-start.3 = (bf16[4,12,6,512]{3,2,1,0:T(8,128)(2,1)S(1)}, bf16[4,12,6,512]{3,2,1,0:T(8,128)(2,1)}, u32[]{:S(2)}, u32[]{:S(2)}) collective-permute-start(bf16[4,12,6,512]{3,2,1,0:T(8,128)(2,1)S(1)} %fusion.152), channel_id=1, source_target_pairs={{0,64},{64,128},{128,192},{1,65},{65,129},{129,193},{2,66},{66,130... | collective-permute-start | bytes 884744 | tf_op jit(solution)/shard_map/while/body/eval_jaxpr/ppermute | solution.py:36
  (19 other events, 18.7 us)
Sparse Core Ops, SparseCore 0:
  10.1 75.8 all-gather.7
  88.8 74.9 all-gather.9
  166.5 74.9 all-gather.11
where the time goes:
time: 682 us; the launch traced here: 675 us
  waiting for transfers between devices  247 us (36%)
  matrix products  141 us (21%)
  local copies, waits for them, and re-layouts  117 us (17%)
  starting transfers between devices  61 us (9%)
  blocking collectives  54.4 us (8%)
  other arithmetic  38.3 us (6%)
  between operations  13.1 us (2%)
    all_gather x1, waiting for transfers between devices, on_device(): lax.all_gather(w_down[0], 'lat', axis=0, tiled=True)  77.8 us
    all_gather x1, waiting for transfers between devices, on_device(): lax.all_gather(w_up[0], 'lat', axis=0, tiled=True)  77.7 us
    all_gather x1, blocking collectives, on_device(): lax.all_gather(w_proj[0], 'lat', axis=0, tiled=True)  54.4 us
    ppermute x14, waiting for transfers between devices, shifted_2(): lax.ppermute(value, axis, [(source, source + steps) for source in range(f...  50.6 us
    dot_general x14, matrix products, attend(): jnp.einsum('abchqk,abckhe->abcqhe', probs, value_heads, preferred_element...  40.9 us
    dot_general x7, matrix products, swin_block(): jnp.dot(hidden, proj_down, preferred_element_type=jnp.float32)  36.4 us
    ppermute x7, starting transfers between devices, padded(): lax.ppermute(head, axis, [((i + 1) % count, i) for i in range(ends)])  29.4 us
    dot_general x14, matrix products, attend(): jnp.einsum('abcqhe,abckhe->abchqk', query_heads, key_heads, preferred_ele...  25.4 us
  transfers between devices with their start and end apart: 31, of which 17 were waited for; matrix products, arithmetic and copies ran while one was open for 11% of the time, Pallas kernels for 0%

commit v1 on v0

v1 whole, which is shorter than its diff:
```python
import jax
import jax.numpy as jnp
from jax import lax
from jax.experimental import pallas as pl
from jax.experimental.pallas import tpu as pltpu
from jax.sharding import PartitionSpec as P

D = 512
LEVELS = 4
HALFROWS = 144
OWN = 288
PER_LEVEL = 36
EPS = 1e-5


def layer_norm(wide, gain):
    center = jnp.mean(wide, axis=-1, keepdims=True)
    moved = wide - center
    spread = jnp.mean(moved * moved, axis=-1, keepdims=True)
    return moved * lax.rsqrt(spread + EPS) * gain


def dot(a, b):
    return jnp.dot(a, b, preferred_element_type=jnp.float32)


def attention(q, k, v, bias, first_lane, ones):
    zero = jnp.zeros_like(q)
    stacked = jnp.concatenate([jnp.where(first_lane, q, zero), jnp.where(first_lane, zero, q)], axis=0)
    scores = lax.dot_general(stacked, k, (((1,), (1,)), ((), ())), preferred_element_type=jnp.float32)
    scores = scores + bias
    top = jnp.max(scores, axis=-1, keepdims=True)
    terms = jnp.exp(scores - top).astype(jnp.bfloat16)
    both = dot(terms, jnp.concatenate([v, ones], axis=1))
    rows = q.shape[0]
    weighed = jnp.where(first_lane, both[:rows, :128], both[rows:, :128])
    total = jnp.where(first_lane, both[:rows, 128:], both[rows:, 128:])
    return (weighed / total).astype(jnp.bfloat16)


def half_bias(shifted, half, has_prev, has_next):
    row = lax.broadcasted_iota(jnp.int32, (HALFROWS, OWN), 0)
    col = lax.broadcasted_iota(jnp.int32, (HALFROWS, OWN), 1)
    far = col >= HALFROWS
    key = jnp.where(far, col - HALFROWS, col)

    def level(i):
        return ((i >= PER_LEVEL).astype(jnp.int32) + (i >= 2 * PER_LEVEL).astype(jnp.int32)
                + (i >= 3 * PER_LEVEL).astype(jnp.int32))

    row_level, key_level = level(row), level(key)
    if shifted:
        group = lambda l: jnp.where(l == 2, 1, l)
        allowed = group(row_level) == group(key_level)
        if half == 0:
            allowed = allowed & (far | (has_prev > 0))
        else:
            allowed = allowed & (jnp.logical_not(far) | (has_next > 0))
    else:
        group = lambda l: (l >= 2).astype(jnp.int32)
        allowed = group(row_level) == group(key_level)
    return jnp.where(allowed, 0.0, -1e30).astype(jnp.float32)


def block_kernel(shifted, joins, wait_weights, edge_ref, refs, gain_ref, w, out_refs, mixed_ref):
    own = refs["own"][...].astype(jnp.float32)
    gain0 = gain_ref[0:1, :]
    normed = layer_norm(own, gain0).astype(jnp.bfloat16)
    if shifted:
        before = layer_norm(refs["prev"][...].astype(jnp.float32), gain0).astype(jnp.bfloat16)
        after = layer_norm(refs["next"][...].astype(jnp.float32), gain0).astype(jnp.bfloat16)
        around = jnp.concatenate([before, normed, after], axis=0)
    else:
        around = normed
    wait_weights("q")
    q = (dot(normed, w["q"]()) ).astype(jnp.bfloat16) * jnp.bfloat16(0.125)
    wait_weights("k")
    k = dot(around, w["k"]()).astype(jnp.bfloat16)
    wait_weights("v")
    v = dot(around, w["v"]()).astype(jnp.bfloat16)
    first_lane = lax.broadcasted_iota(jnp.int32, (HALFROWS, 128), 1) < 64
    ones = jnp.ones((OWN, 128), jnp.bfloat16)
    for half in range(2):
        bias = half_bias(shifted, half, edge_ref[0], edge_ref[1])
        bias = jnp.concatenate([bias, bias], axis=0)
        rows = slice(half * HALFROWS, (half + 1) * HALFROWS)
        start = half * OWN if shifted else 0
        keys = slice(start, start + OWN)
        for pair in range(4):
            cols = slice(pair * 128, (pair + 1) * 128)
            mixed_ref[rows, cols] = attention(q[rows, cols], k[keys, cols], v[keys, cols], bias, first_lane, ones)
    wait_weights("proj")
    residual = own + dot(mixed_ref[...], w["proj"]())
    inner = layer_norm(residual, gain_ref[1:2, :]).astype(jnp.bfloat16)
    total = residual
    for t in range(4):
        wait_weights("up%d" % t)
        hidden = jax.nn.gelu(dot(inner, w["up%d" % t]())).astype(jnp.bfloat16)
        if t == 0:
            wait_weights("down")
        total = total + dot(hidden, w["down"](t))
    result = total.astype(jnp.bfloat16)
    out_refs[0][...] = result
    if joins:
        out_refs[1][...] = (result.astype(jnp.float32) + refs["skip"][...].astype(jnp.float32)).astype(jnp.bfloat16)


ZS, YS = 8, 4
LATS = 2 * ZS * YS
PAIRS = [(0, 3), (1, 2)]


def run_block(weights, x, gains, edges, halo=None, skip=None):
    shifted = halo is not None
    joins = skip is not None
    operands = {"own": x}
    if shifted:
        operands["prev"], operands["next"] = halo
    if joins:
        operands["skip"] = skip
    names = list(operands)
    outs = 2 if joins else 1
    order = ("q", "k", "v", "proj", "up0", "up1", "up2", "up3")

    def body(edge_ref, gain_ref, w_ref, *rest):
        refs = dict(zip(names, rest[: len(names)]))
        out_refs = rest[len(names) : len(names) + outs]
        tiles, mixed, sems = rest[len(names) + outs :]
        copies = {}
        for i, name in enumerate(order):
            copies[name] = pltpu.make_async_copy(w_ref.at[i], tiles.at[i], sems.at[i])
        copies["down"] = pltpu.make_async_copy(w_ref.at[pl.ds(8, 4)], tiles.at[pl.ds(8, 4)], sems.at[8])
        for copy in copies.values():
            copy.start()
        w = {name: (lambda i=i: tiles[i].reshape(D, D)) for i, name in enumerate(order)}
        w["down"] = lambda t: jnp.concatenate(
            [tiles[8 + u, 8 * t + j] for j in range(8) for u in range(4)], axis=0
        )
        block_kernel(shifted, joins, lambda name: copies[name].wait(), edge_ref, refs, gain_ref, w, out_refs, mixed)

    vmem = pl.BlockSpec(memory_space=pltpu.VMEM)
    shape = jax.ShapeDtypeStruct((OWN, D), jnp.bfloat16)
    result = pl.pallas_call(
        body,
        out_shape=(shape,) * outs,
        in_specs=[pl.BlockSpec(memory_space=pltpu.SMEM), vmem, pl.BlockSpec(memory_space=pl.ANY)]
        + [vmem] * len(names),
        out_specs=(vmem,) * outs,
        scratch_shapes=[
            pltpu.VMEM((12, 32, 16, D), jnp.bfloat16),
            pltpu.VMEM((OWN, D), jnp.bfloat16),
            pltpu.SemaphoreType.DMA((9,)),
        ],
        compiler_params=pltpu.CompilerParams(vmem_limit_bytes=32 * 1024 * 1024),
        cost_estimate=pl.CostEstimate(flops=5 * 10**9, bytes_accessed=7 * 10**6, transcendentals=10**6),
    )(edges, gains, weights, *operands.values())
    return result if joins else result[0]


def assemble(place, mine, passed):
    def body(place_ref, *rest):
        out, sems = rest[10], rest[11]
        z0, y0, core = place_ref[0], place_ref[1], place_ref[2]
        copies = []
        for side in range(2):
            source_core = core if side == 0 else 1 - core
            base = 6 * source_core
            for piece, outer in enumerate((0, -1, 1, -2, 2)):
                ref = rest[5 * side + piece]
                inner_first = 2 if piece == 4 else 0
                inner_count = ref.shape[0]
                for n in range(inner_count):
                    inner = inner_first + n
                    parts = ((0, 3, -2), (3, 3, 2)) if inner == 3 else ((0, 6, (0, -1, 1)[inner]),)
                    for first, count, step in parts:
                        for far in range(2):
                            z_step = jnp.where(source_core == 0, step, outer) + 4 * far
                            y_step = jnp.where(source_core == 0, outer, step)
                            chip = lax.rem(z0 + z_step + ZS, ZS) * YS + lax.rem(y0 + y_step + YS, YS)
                            copies.append(
                                pltpu.make_async_copy(
                                    ref.at[n, far, pl.ds(first, count)],
                                    out.at[pl.ds(base + first, count), chip],
                                    sems.at[len(copies)],
                                )
                            )
        for copy in copies:
            copy.start()
        for copy in copies:
            copy.wait()

    anywhere = pl.BlockSpec(memory_space=pl.ANY)
    return pl.pallas_call(
        body,
        out_shape=jax.ShapeDtypeStruct((12, 32, 16, D), jnp.bfloat16),
        in_specs=[pl.BlockSpec(memory_space=pltpu.SMEM)] + [anywhere] * 10,
        out_specs=anywhere,
        scratch_shapes=[pltpu.SemaphoreType.DMA((80,))],
        cost_estimate=pl.CostEstimate(flops=10**6, bytes_accessed=13 * 10**6, transcendentals=0),
    )(place, *mine, *passed)


def lat_id(z, y, core):
    return ((z % ZS) * YS + y % YS) * 2 + core


def moved(along):
    pairs = []
    for z in range(ZS):
        for y in range(YS):
            for core in range(2):
                dz, dy = along(core)
                pairs.append((lat_id(z, y, core), lat_id(z + dz, y + dy, core)))
    return pairs


def ring(level, step):
    return moved(lambda core: (step, 0) if (level == 0) == (core == 0) else (0, step))


SWAP = [(i, i ^ 1) for i in range(LATS)]


def send(value, pairs):
    return lax.ppermute(value, "lat", pairs)


def gather_weights(place, shard):
    both = jnp.stack([shard, send(shard, moved(lambda core: (4, 0)))])
    before, after = send(both, ring(0, 1)), send(both, ring(0, -1))
    far = jnp.concatenate([send(before[:, :3], ring(0, 1)), send(after[:, 3:], ring(0, -1))], axis=1)
    line = jnp.stack([both, before, after, far])
    before, after = send(line, ring(1, 1)), send(line, ring(1, -1))
    mine = [line, before, after, send(before[:2], ring(1, 1)), send(after[2:], ring(1, -1))]
    return assemble(place, mine, [send(piece, SWAP) for piece in mine])


def on_device(tokens, norm_gain, w_qkv, w_proj, w_up, w_down):
    segment = lax.axis_index("segment")
    lat = lax.axis_index("lat")
    core = lat % 2
    even = segment % 2 == 0
    low = (segment == 0) | (segment == 3)
    place = jnp.stack([lat // (2 * YS), (lat // 2) % YS, core]).astype(jnp.int32)
    edges = jnp.stack([lat > 0, lat < LATS - 1]).astype(jnp.int32)

    own = jnp.concatenate(
        [w_qkv[0, :, i * D : (i + 1) * D] for i in range(3)]
        + [w_proj[0]]
        + [w_up[0, :, i * D : (i + 1) * D] for i in range(4)]
        + [w_down[0]],
        axis=0,
    )
    other = send(own, SWAP)
    first, second = jnp.where(core == 0, own, other), jnp.where(core == 0, other, own)
    tall = jnp.stack([first[:64].reshape(8, 8, D), second[:64].reshape(8, 8, D)], axis=1).reshape(8, 16, D)
    tall = jnp.concatenate([tall, first[64:].reshape(2, 16, D), second[64:].reshape(2, 16, D)], axis=0)
    shard = jnp.where(core == 0, tall[:6], tall[6:])
    beside = [(0, 1), (1, 0), (2, 3), (3, 2)]
    other = lax.ppermute(shard, "segment", beside)
    other_gain = lax.ppermute(norm_gain[0], "segment", beside)
    weights = [
        gather_weights(place, jnp.where(even, shard, other)),
        gather_weights(place, jnp.where(even, other, shard)),
    ]
    gains = [jnp.where(even, norm_gain[0], other_gain), jnp.where(even, other_gain, norm_gain[0])]

    fields = jnp.where(low, tokens[:2], tokens[2:])
    fields = fields.reshape(2, LEVELS, 2, 6, 6, D).transpose(0, 2, 1, 3, 4, 5).reshape(2, OWN, D)

    def halo(field):
        up = send(field[HALFROWS:], [(i, i + 1) for i in range(LATS - 1)])
        down = send(field[:HALFROWS], [(i + 1, i) for i in range(LATS - 1)])
        return up, down

    def pass_on(value, pairs):
        return lax.ppermute(value, "segment", pairs)

    pair = range(2)
    a0 = [run_block(weights[0], fields[m], gains[0], edges) for m in pair]
    a1 = [run_block(weights[1], a0[m], gains[1], edges, halo=halo(a0[m])) for m in pair]
    skips = [pass_on(a0[m], PAIRS) for m in pair]
    entering = [pass_on(a1[m], PAIRS) for m in pair]
    a2, a3 = [], []
    for m in pair:
        out, joined = run_block(weights[0], entering[m], gains[0], edges, skip=skips[m])
        a2.append((out, joined))
    for m in pair:
        a3.append(run_block(weights[1], a2[m][1], gains[1], edges, halo=halo(a2[m][1])))
    a2 = [out for out, _ in a2]

    def select(b0, b1, b2, b3):
        return jnp.where(segment == 0, b0, jnp.where(segment == 1, b1, jnp.where(segment == 2, b2, b3)))

    kept, got = [], []
    for m in pair:
        kept.append(select(a0[m], a1[m], a2[m], a3[m]))
        got.append(
            select(
                pass_on(a0[m], [(1, 0)]),
                pass_on(a1[m], [(0, 1)]),
                pass_on(a2[m], [(3, 2)]),
                pass_on(a3[m], [(2, 3)]),
            )
        )
    outs = [jnp.where(low, kept[m], got[m]) for m in pair] + [jnp.where(low, got[m], kept[m]) for m in pair]
    out = jnp.stack(outs).reshape(4, 2, LEVELS, 6, 6, D).transpose(0, 2, 1, 3, 4, 5)
    return out.reshape(1, 4, LEVELS, 12, 6, D)


def solution(mesh):
    return jax.shard_map(
        on_device,
        mesh=mesh,
        in_specs=(
            P(None, None, "lat", None, None),
            P("segment", None, None),
            P("segment", "lat", None),
            P("segment", "lat", None),
            P("segment", "lat", None),
            P("segment", "lat", None),
        ),
        out_specs=P("segment", None, None, "lat", None, None),
        check_vma=False,
    )
```

time: 682 us -> 612 us (0.90)
  Pallas kernels: 0 us -> 445 us
  waiting for transfers between devices: 247 us -> 41.2 us
  matrix products: 141 us -> 0 us
  local copies, waits for them, and re-layouts: 117 us -> 22.3 us
  blocking collectives: 54.4 us -> 0 us
  other arithmetic: 38.3 us -> 3.02 us
  starting transfers between devices: 61 us -> 89.8 us
  between operations: 13.1 us -> 1.29 us
    pallas_call x0 -> x10, Pallas kernels: none -> 445 us  [the longest x2 386 us: assemble(): pl.pallas_call(body, out_shape=jax.ShapeDtypeStruct((12, 32, 16, D), jnp....]
    all_gather x3 -> x0, waiting for transfers between devices: 178 us -> none  [the longest x1 77.8 us: on_device(): lax.all_gather(w_down[0], 'lat', axis=0, tiled=True)]
    dot_general x49 -> x0, matrix products: 123 us -> none  [the longest x14 40.9 us: attend(): jnp.einsum('abchqk,abckhe->abcqhe', probs, value_heads, preferred_element...]
    all_gather x1 -> x0, blocking collectives: 54.4 us -> none  [on_device(): lax.all_gather(w_proj[0], 'lat', axis=0, tiled=True)]
    slice x112 -> x15, local copies, waits for them, and re-layouts: 43 us -> 6.05 us  [the longest x2 2.58 us: gather_weights(): before[:2]]
    ppermute x28 -> x51, starting transfers between devices: 60.9 us -> 89.8 us  [the longest x37 66.7 us: send(): return lax.ppermute(value, 'lat', pairs)]
    dynamic_slice x28 -> x0, local copies, waits for them, and re-layouts: 28.4 us -> none  [the longest x7 12.6 us: tick(): previous = lax.dynamic_index_in_dim(outputs, work_slot, 0, keepdims=False)]
    ppermute x28 -> x51, waiting for transfers between devices: 66.8 us -> 41.2 us  [the longest x37 25.8 us: send(): return lax.ppermute(value, 'lat', pairs)]
  transfers between devices with their start and end apart: 31 -> 51, of which waited for: 17 -> 14; matrix products, arithmetic and copies ran while one was open for 11% -> 1% of each run, Pallas kernels for 0% -> 74%
where the time goes in v1:
time: 612 us; the launch traced here: 602 us
  Pallas kernels  445 us (73%)
  starting transfers between devices  89.8 us (15%)
  waiting for transfers between devices  41.2 us (7%)
  local copies, waits for them, and re-layouts  22.3 us (4%)
    pallas_call x2, Pallas kernels, assemble(): pl.pallas_call(body, out_shape=jax.ShapeDtypeStruct((12, 32, 16, D), jnp....  386 us
    ppermute x37, starting transfers between devices, send(): return lax.ppermute(value, 'lat', pairs)  66.7 us
    pallas_call x8, Pallas kernels, run_block(): pl.pallas_call(body, out_shape=(shape,) * outs, in_specs=[pl.BlockSpec(me...  58.6 us
    ppermute x37, waiting for transfers between devices, send(): return lax.ppermute(value, 'lat', pairs)  25.8 us
    ppermute x12, starting transfers between devices, pass_on(): return lax.ppermute(value, 'segment', pairs)  21.4 us
  transfers between devices with their start and end apart: 51, of which 14 were waited for; matrix products, arithmetic and copies ran while one was open for 1% of the time, Pallas kernels for 74%

profile of v1, /device:TPU:134, one launch (start us, length us, event | category | flops | bytes accessed | tf_op | source)
XLA Modules:
  0.0 602.4 jit_solution(2649434542569041607)
XLA Ops:
  8.7 4.0 collective-permute-done.2
  12.8 5.9 collective-permute-start.3
  18.7 5.6 collective-permute-done.17
  24.3 2.8 collective-permute-start.18
  27.7 1.6 collective-permute-start.4
  29.3 1.7 collective-permute-start.5
  31.3 1.6 collective-permute-start.20
  32.9 1.8 collective-permute-start.21
  35.1 3.0 collective-permute-start.7
  38.3 2.0 collective-permute-start.22
  40.3 1.5 collective-permute-done.6
  41.9 2.0 collective-permute-start.8
  45.2 1.8 collective-permute-start.23
  47.3 4.3 collective-permute-done.22.rest_1_
  53.2 6.9 %collective-permute-done.8.rest_1_ = bf16[4,2,6,16,512]{4,3,2,1,0:T(8,128)(2,1)} collective-permute-done((bf16[4,2,6,16,512]{4,3,2,1,0:T(8,128)(2,1)S(1)}, bf16[4,2,6,16,512]{4,3,2,1,0:T(8,128)(2,1)}, u32[]{:S(2)}, u32[]{:S(2)}) %collective-permute-start.8) | collective-permute-done | bytes 786464 | tf_op jit(solution)/shard_map/ppermute | solution.py:225
  60.8 1.8 slice.146
  62.6 1.9 collective-permute-start.10
  64.5 1.8 slice.147
  70.8 1.4 collective-permute-start.25
  75.0 3.7 collective-permute-done.25.rest_4_
  81.0 193.1 %shard_map.64.w_ref = bf16[12,32,16,512]{3,2,1,0:T(8,128)(2,1)} custom-call(s32[3]{0:T(128)} %pad_add_fusion.place_ref, bf16[4,2,6,16,512]{4,3,2,1,0:T(8,128)(2,1)} %copy-done.4, bf16[4,2,6,16,512]{4,3,2,1,0:T(8,128)(2,1)} %collective-permute-done.8.rest_1_, bf16[4,2,6,16,512]{4,3,2,1,0:T(8,128)(2,1)} %collective-permute-done.9.rest_2_, ...), custom_call_target="tpu_custom_call" | custom-call | flops 1000000 | bytes 13000000 | tf_op jit(solution)/shard_map/pallas_call | solution.py:193
  274.1 2.8 copy-done
  276.9 7.1 %shard_map.65.rest_0_ = bf16[288,512]{1,0:T(8,128)(2,1)S(1)} custom-call(s32[2]{0:T(128)S(1)} %add_convert_fusion.edge_ref, f32[2,512]{1,0:T(2,128)S(1)} %get-tuple-element.38.gain_ref, bf16[12,32,16,512]{3,2,1,0:T(8,128)(2,1)S(1)} %copy-done, bf16[288,512]{1,0:T(8,128)(2,1)S(1)} %squeeze.48.rest_0_), custom_call_target="tpu_custom_call" | custom-call | flops 5000000000 | bytes 7000000 | tf_op jit(solution)/shard_map/pallas_call | solution.py:143
  284.7 7.1 %shard_map.70.rest_0_ = bf16[288,512]{1,0:T(8,128)(2,1)S(1)} custom-call(s32[2]{0:T(128)S(1)} %add_convert_fusion.edge_ref, f32[2,512]{1,0:T(2,128)S(1)} %get-tuple-element.38.gain_ref, bf16[12,32,16,512]{3,2,1,0:T(8,128)(2,1)S(1)} %copy-done, bf16[288,512]{1,0:T(8,128)(2,1)S(1)} %squeeze.49.rest_0_), custom_call_target="tpu_custom_call" | custom-call | flops 5000000000 | bytes 7000000 | tf_op jit(solution)/shard_map/pallas_call | solution.py:143
  293.9 2.0 collective-permute-start.31
  295.8 6.9 %collective-permute-start.32 = (bf16[144,512]{1,0:T(8,128)(2,1)}, bf16[144,512]{1,0:T(8,128)(2,1)S(1)}, u32[]{:S(2)}, u32[]{:S(2)}) collective-permute-start(bf16[144,512]{1,0:T(8,128)(2,1)} %get-tuple-element.23), channel_id=1, source_target_pairs={{1,0},{2,1},{3,2},{4,3},{5,4},{6,5},{7,6},{8,7},{9,8},{10,9},{11,1... | collective-permute-start | bytes 442376 | tf_op jit(solution)/shard_map/ppermute | solution.py:225
  304.1 193.1 %shard_map.66.w_ref = bf16[12,32,16,512]{3,2,1,0:T(8,128)(2,1)} custom-call(s32[3]{0:T(128)} %pad_add_fusion.place_ref, bf16[4,2,6,16,512]{4,3,2,1,0:T(8,128)(2,1)} %copy-done.3, bf16[4,2,6,16,512]{4,3,2,1,0:T(8,128)(2,1)} %copy-done.5, bf16[4,2,6,16,512]{4,3,2,1,0:T(8,128)(2,1)} %copy-done.7, bf16[2,2,6,16,512]{4,3,2,1,0:T(8,128)(2,1)} %collective-permute-done.24.rest_3_, ...), custom_call_target="tpu_custom_call" | custom-call | flops 1000000 | bytes 13000000 | tf_op jit(solution)/shard_map/pallas_call | solution.py:193
  497.2 1.9 collective-permute-start.41
  499.2 7.1 %collective-permute-start.42 = (bf16[144,512]{1,0:T(8,128)(2,1)S(1)}, bf16[144,512]{1,0:T(8,128)(2,1)S(1)}, u32[]{:S(2)}, u32[]{:S(2)}) collective-permute-start(bf16[144,512]{1,0:T(8,128)(2,1)S(1)} %get-tuple-element.27), channel_id=1, source_target_pairs={{1,0},{2,1},{3,2},{4,3},{5,4},{6,5},{7,6},{8,7},{9,8},{10,9},{11,1... | collective-permute-start | bytes 442376 | tf_op jit(solution)/shard_map/ppermute | solution.py:225
  506.3 2.8 copy-done.1
  509.1 7.5 %shard_map.67 = bf16[288,512]{1,0:T(8,128)(2,1)S(1)} custom-call(s32[2]{0:T(128)S(1)} %add_convert_fusion.edge_ref, f32[2,512]{1,0:T(2,128)S(1)} %get-tuple-element.37.gain_ref, bf16[12,32,16,512]{3,2,1,0:T(8,128)(2,1)S(1)} %copy-done.1, bf16[288,512]{1,0:T(8,128)(2,1)S(1)} %shard_map.65.rest_0_, bf16[144,512]{1,0:T(8,128)(2,1)S(1)} %collective-permute-done.31.rest_1_, ...), custom_call_target="tpu_custom_call" | custom-call | flops 5000000000 | bytes 7000000 | tf_op jit(solution)/shard_map/pallas_call | solution.py:143
  516.6 1.5 collective-permute-start.47
  519.4 7.5 %shard_map.71 = bf16[288,512]{1,0:T(8,128)(2,1)S(1)} custom-call(s32[2]{0:T(128)S(1)} %add_convert_fusion.edge_ref, f32[2,512]{1,0:T(2,128)S(1)} %get-tuple-element.37.gain_ref, bf16[12,32,16,512]{3,2,1,0:T(8,128)(2,1)S(1)} %copy-done.2, bf16[288,512]{1,0:T(8,128)(2,1)S(1)} %shard_map.70.rest_0_, bf16[144,512]{1,0:T(8,128)(2,1)S(1)} %collective-permute-done.41.rest_1_, ...), custom_call_target="tpu_custom_call" | custom-call | flops 5000000000 | bytes 7000000 | tf_op jit(solution)/shard_map/pallas_call | solution.py:143
  528.6 1.5 collective-permute-start.43
  530.1 7.1 %shard_map.68 = (bf16[288,512]{1,0:T(8,128)(2,1)S(1)}, bf16[288,512]{1,0:T(8,128)(2,1)S(1)}) custom-call(s32[2]{0:T(128)S(1)} %add_convert_fusion.edge_ref, f32[2,512]{1,0:T(2,128)S(1)} %get-tuple-element.38.gain_ref, bf16[12,32,16,512]{3,2,1,0:T(8,128)(2,1)S(1)} %bitcast.66, bf16[288,512]{1,0:T(8,128)(2,1)S(1)} %collective-permute-done.33.rest_0_, ...), custom_call_target="tpu_custom_call" | custom-call | flops 5000000000 | bytes 7000000 | tf_op jit(solution)/shard_map/pallas_call | solution.py:143
  537.3 1.9 collective-permute-start.35
  539.2 3.5 collective-permute-done.43.rest_0_
  542.7 3.5 collective-permute-start.36
  546.2 7.1 %shard_map.72 = (bf16[288,512]{1,0:T(8,128)(2,1)S(1)}, bf16[288,512]{1,0:T(8,128)(2,1)S(1)}) custom-call(s32[2]{0:T(128)S(1)} %add_convert_fusion.edge_ref, f32[2,512]{1,0:T(2,128)S(1)} %get-tuple-element.38.gain_ref, bf16[12,32,16,512]{3,2,1,0:T(8,128)(2,1)S(1)} %bitcast.66, bf16[288,512]{1,0:T(8,128)(2,1)S(1)} %collective-permute-done.43.rest_0_, ...), custom_call_target="tpu_custom_call" | custom-call | flops 5000000000 | bytes 7000000 | tf_op jit(solution)/shard_map/pallas_call | solution.py:143
  553.4 1.9 collective-permute-start.45
  555.3 7.2 %collective-permute-start.46 = (bf16[144,512]{1,0:T(8,128)(2,1)S(1)}, bf16[144,512]{1,0:T(8,128)(2,1)S(1)}, u32[]{:S(2)}, u32[]{:S(2)}) collective-permute-start(bf16[144,512]{1,0:T(8,128)(2,1)S(1)} %get-tuple-element.25), channel_id=1, source_target_pairs={{1,0},{2,1},{3,2},{4,3},{5,4},{6,5},{7,6},{8,7},{9,8},{10,9},{11,1... | collective-permute-start | bytes 442376 | tf_op jit(solution)/shard_map/ppermute | solution.py:225
  562.5 7.5 %shard_map.69 = bf16[288,512]{1,0:T(8,128)(2,1)S(1)} custom-call(s32[2]{0:T(128)S(1)} %add_convert_fusion.edge_ref, f32[2,512]{1,0:T(2,128)S(1)} %get-tuple-element.37.gain_ref, bf16[12,32,16,512]{3,2,1,0:T(8,128)(2,1)S(1)} %copy-done.2, bf16[288,512]{1,0:T(8,128)(2,1)S(1)} %get-tuple-element.10.rest_0_, ...), custom_call_target="tpu_custom_call" | custom-call | flops 5000000000 | bytes 7000000 | tf_op jit(solution)/shard_map/pallas_call | solution.py:143
  570.1 4.6 collective-permute-start.39
  576.0 7.5 %shard_map.73 = bf16[288,512]{1,0:T(8,128)(2,1)S(1)} custom-call(s32[2]{0:T(128)S(1)} %add_convert_fusion.edge_ref, f32[2,512]{1,0:T(2,128)S(1)} %get-tuple-element.37.gain_ref, bf16[12,32,16,512]{3,2,1,0:T(8,128)(2,1)S(1)} %copy-done.2, bf16[288,512]{1,0:T(8,128)(2,1)S(1)} %get-tuple-element.12.rest_0_, ...), custom_call_target="tpu_custom_call" | custom-call | flops 5000000000 | bytes 7000000 | tf_op jit(solution)/shard_map/pallas_call | solution.py:143
  584.3 5.3 collective-permute-start.49
  591.3 1.8 collective-permute-done.49
  593.1 5.2 collective-permute-done.50
  600.1 1.9 copy.17
  (145 shorter events, 36.0 us)
Async XLA Ops:
  12.7 11.6 %collective-permute-start.17 = (bf16[6,16,512]{2,1,0:T(8,128)(2,1)S(1)}, bf16[6,16,512]{2,1,0:T(8,128)(2,1)S(1)}, u32[]{:S(2)}, u32[]{:S(2)}) collective-permute-start(bf16[6,16,512]{2,1,0:T(8,128)(2,1)S(1)} %get-tuple-element.31), channel_id=1, source_target_pairs={{0,32},{1,33},{2,34},{3,35},{4,36},{5,37},{6,38},{7,39},{8,40},{9,... | collective-permute-start | bytes 294920 | tf_op jit(solution)/shard_map/ppermute | solution.py:225
  12.8 14.8 %collective-permute-start.3 = (bf16[6,16,512]{2,1,0:T(8,128)(2,1)S(1)}, bf16[6,16,512]{2,1,0:T(8,128)(2,1)S(1)}, u32[]{:S(2)}, u32[]{:S(2)}) collective-permute-start(bf16[6,16,512]{2,1,0:T(8,128)(2,1)S(1)} %get-tuple-element.32), channel_id=1, source_target_pairs={{0,32},{1,33},{2,34},{3,35},{4,36},{5,37},{6,38},{7,39},{8,40},{9,... | collective-permute-start | bytes 294920 | tf_op jit(solution)/shard_map/ppermute | solution.py:225
  24.3 7.0 %collective-permute-start.18 = (bf16[2,6,16,512]{3,2,1,0:T(8,128)(2,1)S(1)}, bf16[2,6,16,512]{3,2,1,0:T(8,128)(2,1)S(1)}, u32[]{:S(2)}, u32[]{:S(2)}) collective-permute-start(bf16[2,6,16,512]{3,2,1,0:T(8,128)(2,1)S(1)} %get-tuple-element.30), channel_id=1, source_target_pairs={{0,8},{1,3},{2,10},{3,5},{4,12},{5,7},{6,14},{7,1},{8,16},{9,11},{... | collective-permute-start | bytes 589832 | tf_op jit(solution)/shard_map/ppermute | solution.py:225
  27.1 5.8 collective-permute-start.19
  27.7 7.0 %collective-permute-start.4 = (bf16[2,6,16,512]{3,2,1,0:T(8,128)(2,1)S(1)}, bf16[2,6,16,512]{3,2,1,0:T(8,128)(2,1)S(1)}, u32[]{:S(2)}, u32[]{:S(2)}) collective-permute-start(bf16[2,6,16,512]{3,2,1,0:T(8,128)(2,1)S(1)} %get-tuple-element.34), channel_id=1, source_target_pairs={{0,8},{1,3},{2,10},{3,5},{4,12},{5,7},{6,14},{7,1},{8,16},{9,11},{... | collective-permute-start | bytes 589832 | tf_op jit(solution)/shard_map/ppermute | solution.py:225
  29.3 5.8 collective-permute-start.5
  31.3 6.9 %collective-permute-start.20 = (bf16[2,3,16,512]{3,2,1,0:T(8,128)(2,1)S(1)}, bf16[2,3,16,512]{3,2,1,0:T(8,128)(2,1)S(1)}, u32[]{:S(2)}, u32[]{:S(2)}) collective-permute-start(bf16[2,3,16,512]{3,2,1,0:T(8,128)(2,1)S(1)} %slice.149), channel_id=1, source_target_pairs={{0,8},{1,3},{2,10},{3,5},{4,12},{5,7},{6,14},{7,1},{8,16},{9,11},{... | collective-permute-start | bytes 294920 | tf_op jit(solution)/shard_map/ppermute | solution.py:225
  32.9 5.3 collective-permute-start.21
  34.7 7.0 %collective-permute-start.6 = (bf16[2,3,16,512]{3,2,1,0:T(8,128)(2,1)S(1)}, bf16[2,3,16,512]{3,2,1,0:T(8,128)(2,1)S(1)}, u32[]{:S(2)}, u32[]{:S(2)}) collective-permute-start(bf16[2,3,16,512]{3,2,1,0:T(8,128)(2,1)S(1)} %slice.144), channel_id=1, source_target_pairs={{0,8},{1,3},{2,10},{3,5},{4,12},{5,7},{6,14},{7,1},{8,16},{9,11},{... | collective-permute-start | bytes 294920 | tf_op jit(solution)/shard_map/ppermute | solution.py:225
  35.1 6.6 %collective-permute-start.7 = (bf16[2,3,16,512]{3,2,1,0:T(8,128)(2,1)S(1)}, bf16[2,3,16,512]{3,2,1,0:T(8,128)(2,1)S(1)}, u32[]{:S(2)}, u32[]{:S(2)}) collective-permute-start(bf16[2,3,16,512]{3,2,1,0:T(8,128)(2,1)S(1)} %slice.145), channel_id=1, source_target_pairs={{0,56},{1,7},{2,58},{3,1},{4,60},{5,3},{6,62},{7,5},{8,0},{9,15},{... | collective-permute-start | bytes 294920 | tf_op jit(solution)/shard_map/ppermute | solution.py:225
  38.3 13.3 %collective-permute-start.22 = (bf16[4,2,6,16,512]{4,3,2,1,0:T(8,128)(2,1)S(1)}, bf16[4,2,6,16,512]{4,3,2,1,0:T(8,128)(2,1)S(1)}, u32[]{:S(2)}, u32[]{:S(2)}) collective-permute-start(bf16[4,2,6,16,512]{4,3,2,1,0:T(8,128)(2,1)S(1)} %pad_maximum_fusion.1.rest_0_), channel_id=1, source_target_pairs={{0,2},{1,9},{2,4},{3,11},{4,6},{5,13},{6,0},{7,15},{8,10},{9,17},{... | collective-permute-start | bytes 2359304 | tf_op jit(solution)/shard_map/ppermute | solution.py:225
  41.9 18.2 %collective-permute-start.8 = (bf16[4,2,6,16,512]{4,3,2,1,0:T(8,128)(2,1)S(1)}, bf16[4,2,6,16,512]{4,3,2,1,0:T(8,128)(2,1)}, u32[]{:S(2)}, u32[]{:S(2)}) collective-permute-start(bf16[4,2,6,16,512]{4,3,2,1,0:T(8,128)(2,1)S(1)} %pad_maximum_fusion.rest_0_), channel_id=1, source_target_pairs={{0,2},{1,9},{2,4},{3,11},{4,6},{5,13},{6,0},{7,15},{8,10},{9,17},{... | collective-permute-start | bytes 2359304 | tf_op jit(solution)/shard_map/ppermute | solution.py:225
  43.9 18.7 %collective-permute-start.9 = (bf16[4,2,6,16,512]{4,3,2,1,0:T(8,128)(2,1)S(1)}, bf16[4,2,6,16,512]{4,3,2,1,0:T(8,128)(2,1)}, u32[]{:S(2)}, u32[]{:S(2)}) collective-permute-start(bf16[4,2,6,16,512]{4,3,2,1,0:T(8,128)(2,1)S(1)} %pad_maximum_fusion.rest_0_), channel_id=1, source_target_pairs={{0,6},{1,57},{2,0},{3,59},{4,2},{5,61},{6,4},{7,63},{8,14},{9,1},{... | collective-permute-start | bytes 2359304 | tf_op jit(solution)/shard_map/ppermute | solution.py:225
  45.2 22.4 %collective-permute-start.23 = (bf16[4,2,6,16,512]{4,3,2,1,0:T(8,128)(2,1)S(1)}, bf16[4,2,6,16,512]{4,3,2,1,0:T(8,128)(2,1)S(1)}, u32[]{:S(2)}, u32[]{:S(2)}) collective-permute-start(bf16[4,2,6,16,512]{4,3,2,1,0:T(8,128)(2,1)S(1)} %pad_maximum_fusion.1.rest_0_), channel_id=1, source_target_pairs={{0,6},{1,57},{2,0},{3,59},{4,2},{5,61},{6,4},{7,63},{8,14},{9,1},{... | collective-permute-start | bytes 2359304 | tf_op jit(solution)/shard_map/ppermute | solution.py:225
  47.0 20.7 %collective-permute-start.12 = (bf16[4,2,6,16,512]{4,3,2,1,0:T(8,128)(2,1)S(1)}, bf16[4,2,6,16,512]{4,3,2,1,0:T(8,128)(2,1)}, u32[]{:S(2)}, u32[]{:S(2)}) collective-permute-start(bf16[4,2,6,16,512]{4,3,2,1,0:T(8,128)(2,1)S(1)} %pad_maximum_fusion.rest_0_), channel_id=1, source_target_pairs={{0,1},{1,0},{2,3},{3,2},{4,5},{5,4},{6,7},{7,6},{8,9},{9,8},{10,11... | collective-permute-start | bytes 2359304 | tf_op jit(solution)/shard_map/ppermute | solution.py:225
  51.6 14.7 %collective-permute-start = (f32[2,512]{1,0:T(2,128)S(1)}, f32[2,512]{1,0:T(2,128)S(1)}, u32[]{:S(2)}, u32[]{:S(2)}) collective-permute-start(f32[2,512]{1,0:T(2,128)S(1)} %bitcast.79), channel_id=1, source_target_pairs={{0,64},{64,0},{128,192},{192,128},{1,65},{65,1},{129,193},{193,129... | collective-permute-start | bytes 12296 | tf_op jit(solution)/shard_map/ppermute | solution.py:261
  60.1 10.6 %collective-permute-start.24 = (bf16[2,2,6,16,512]{4,3,2,1,0:T(8,128)(2,1)}, bf16[2,2,6,16,512]{4,3,2,1,0:T(8,128)(2,1)}, u32[]{:S(2)}, u32[]{:S(2)}) collective-permute-start(bf16[2,2,6,16,512]{4,3,2,1,0:T(8,128)(2,1)} %slice.151), channel_id=1, source_target_pairs={{0,2},{1,9},{2,4},{3,11},{4,6},{5,13},{6,0},{7,15},{8,10},{9,17},{... | collective-permute-start | bytes 1179656 | tf_op jit(solution)/shard_map/ppermute | solution.py:225
  62.6 11.1 %collective-permute-start.10 = (bf16[2,2,6,16,512]{4,3,2,1,0:T(8,128)(2,1)}, bf16[2,2,6,16,512]{4,3,2,1,0:T(8,128)(2,1)}, u32[]{:S(2)}, u32[]{:S(2)}) collective-permute-start(bf16[2,2,6,16,512]{4,3,2,1,0:T(8,128)(2,1)} %slice.146), channel_id=1, source_target_pairs={{0,2},{1,9},{2,4},{3,11},{4,6},{5,13},{6,0},{7,15},{8,10},{9,17},{... | collective-permute-start | bytes 1179656 | tf_op jit(solution)/shard_map/ppermute | solution.py:225
  66.3 8.1 %collective-permute-start.11 = (bf16[2,2,6,16,512]{4,3,2,1,0:T(8,128)(2,1)}, bf16[2,2,6,16,512]{4,3,2,1,0:T(8,128)(2,1)}, u32[]{:S(2)}, u32[]{:S(2)}) collective-permute-start(bf16[2,2,6,16,512]{4,3,2,1,0:T(8,128)(2,1)} %slice.147), channel_id=1, source_target_pairs={{0,6},{1,57},{2,0},{3,59},{4,2},{5,61},{6,4},{7,63},{8,14},{9,1},{... | collective-permute-start | bytes 1179656 | tf_op jit(solution)/shard_map/ppermute | solution.py:225
  67.7 11.9 %collective-permute-start.13 = (bf16[4,2,6,16,512]{4,3,2,1,0:T(8,128)(2,1)}, bf16[4,2,6,16,512]{4,3,2,1,0:T(8,128)(2,1)}, u32[]{:S(2)}, u32[]{:S(2)}) collective-permute-start(bf16[4,2,6,16,512]{4,3,2,1,0:T(8,128)(2,1)} %collective-permute-done.8.rest_1_), channel_id=1, source_target_pairs={{0,1},{1,0},{2,3},{3,2},{4,5},{5,4},{6,7},{7,6},{8,9},{9,8},{10,11... | collective-permute-start | bytes 2359304 | tf_op jit(solution)/shard_map/ppermute | solution.py:225
  67.7 12.5 %collective-permute-start.14 = (bf16[4,2,6,16,512]{4,3,2,1,0:T(8,128)(2,1)}, bf16[4,2,6,16,512]{4,3,2,1,0:T(8,128)(2,1)}, u32[]{:S(2)}, u32[]{:S(2)}) collective-permute-start(bf16[4,2,6,16,512]{4,3,2,1,0:T(8,128)(2,1)} %collective-permute-done.9.rest_2_), channel_id=1, source_target_pairs={{0,1},{1,0},{2,3},{3,2},{4,5},{5,4},{6,7},{7,6},{8,9},{9,8},{10,11... | collective-permute-start | bytes 2359304 | tf_op jit(solution)/shard_map/ppermute | solution.py:225
  70.8 8.0 %collective-permute-start.25 = (bf16[2,2,6,16,512]{4,3,2,1,0:T(8,128)(2,1)S(1)}, bf16[2,2,6,16,512]{4,3,2,1,0:T(8,128)(2,1)}, u32[]{:S(2)}, u32[]{:S(2)}) collective-permute-start(bf16[2,2,6,16,512]{4,3,2,1,0:T(8,128)(2,1)S(1)} %slice.152), channel_id=1, source_target_pairs={{0,6},{1,57},{2,0},{3,59},{4,2},{5,61},{6,4},{7,63},{8,14},{9,1},{... | collective-permute-start | bytes 1179656 | tf_op jit(solution)/shard_map/ppermute | solution.py:225
  73.7 5.1 collective-permute-start.15
  78.8 213.1 %collective-permute-start.26 = (bf16[4,2,6,16,512]{4,3,2,1,0:T(8,128)(2,1)S(1)}, bf16[4,2,6,16,512]{4,3,2,1,0:T(8,128)(2,1)}, u32[]{:S(2)}, u32[]{:S(2)}) collective-permute-start(bf16[4,2,6,16,512]{4,3,2,1,0:T(8,128)(2,1)S(1)} %pad_maximum_fusion.1.rest_0_), channel_id=1, source_target_pairs={{0,1},{1,0},{2,3},{3,2},{4,5},{5,4},{6,7},{7,6},{8,9},{9,8},{10,11... | collective-permute-start | bytes 2359304 | tf_op jit(solution)/shard_map/ppermute | solution.py:225
  78.8 217.0 %collective-permute-start.27 = (bf16[4,2,6,16,512]{4,3,2,1,0:T(8,128)(2,1)S(1)}, bf16[4,2,6,16,512]{4,3,2,1,0:T(8,128)(2,1)}, u32[]{:S(2)}, u32[]{:S(2)}) collective-permute-start(bf16[4,2,6,16,512]{4,3,2,1,0:T(8,128)(2,1)S(1)} %copy-done.6), channel_id=1, source_target_pairs={{0,1},{1,0},{2,3},{3,2},{4,5},{5,4},{6,7},{7,6},{8,9},{9,8},{10,11... | collective-permute-start | bytes 2359304 | tf_op jit(solution)/shard_map/ppermute | solution.py:225
  79.4 223.4 %collective-permute-start.28 = (bf16[4,2,6,16,512]{4,3,2,1,0:T(8,128)(2,1)S(1)}, bf16[4,2,6,16,512]{4,3,2,1,0:T(8,128)(2,1)}, u32[]{:S(2)}, u32[]{:S(2)}) collective-permute-start(bf16[4,2,6,16,512]{4,3,2,1,0:T(8,128)(2,1)S(1)} %collective-permute-done.23.rest_2_), channel_id=1, source_target_pairs={{0,1},{1,0},{2,3},{3,2},{4,5},{5,4},{6,7},{7,6},{8,9},{9,8},{10,11... | collective-permute-start | bytes 2359304 | tf_op jit(solution)/shard_map/ppermute | solution.py:225
  80.1 213.0 %collective-permute-start.29 = (bf16[2,2,6,16,512]{4,3,2,1,0:T(8,128)(2,1)}, bf16[2,2,6,16,512]{4,3,2,1,0:T(8,128)(2,1)}, u32[]{:S(2)}, u32[]{:S(2)}) collective-permute-start(bf16[2,2,6,16,512]{4,3,2,1,0:T(8,128)(2,1)} %collective-permute-done.24.rest_3_), channel_id=1, source_target_pairs={{0,1},{1,0},{2,3},{3,2},{4,5},{5,4},{6,7},{7,6},{8,9},{9,8},{10,11... | collective-permute-start | bytes 1179656 | tf_op jit(solution)/shard_map/ppermute | solution.py:225
  80.2 213.7 %collective-permute-start.30 = (bf16[2,2,6,16,512]{4,3,2,1,0:T(8,128)(2,1)}, bf16[2,2,6,16,512]{4,3,2,1,0:T(8,128)(2,1)}, u32[]{:S(2)}, u32[]{:S(2)}) collective-permute-start(bf16[2,2,6,16,512]{4,3,2,1,0:T(8,128)(2,1)} %collective-permute-done.25.rest_4_), channel_id=1, source_target_pairs={{0,1},{1,0},{2,3},{3,2},{4,5},{5,4},{6,7},{7,6},{8,9},{9,8},{10,11... | collective-permute-start | bytes 1179656 | tf_op jit(solution)/shard_map/ppermute | solution.py:225
  291.9 235.1 %collective-permute-start.34 = (bf16[288,512]{1,0:T(8,128)(2,1)S(1)}, bf16[288,512]{1,0:T(8,128)(2,1)S(1)}, u32[]{:S(2)}, u32[]{:S(2)}) collective-permute-start(bf16[288,512]{1,0:T(8,128)(2,1)S(1)} %shard_map.65.rest_0_), channel_id=1, source_target_pairs={{0,192},{64,128},{1,193},{65,129},{2,194},{66,130},{3,195},{67,131... | collective-permute-start | bytes 884744 | tf_op jit(solution)/shard_map/ppermute | solution.py:277
  293.2 290.4 %collective-permute-start.37 = (bf16[288,512]{1,0:T(8,128)(2,1)S(1)}, bf16[288,512]{1,0:T(8,128)(2,1)S(1)}, u32[]{:S(2)}, u32[]{:S(2)}) collective-permute-start(bf16[288,512]{1,0:T(8,128)(2,1)S(1)} %shard_map.65.rest_0_), channel_id=1, source_target_pairs={{64,0},{65,1},{66,2},{67,3},{68,4},{69,5},{70,6},{71,7},{72,8},{73... | collective-permute-start | bytes 884744 | tf_op jit(solution)/shard_map/ppermute | solution.py:277
  293.9 203.3 %collective-permute-start.31 = (bf16[144,512]{1,0:T(8,128)(2,1)}, bf16[144,512]{1,0:T(8,128)(2,1)S(1)}, u32[]{:S(2)}, u32[]{:S(2)}) collective-permute-start(bf16[144,512]{1,0:T(8,128)(2,1)} %get-tuple-element.24), channel_id=1, source_target_pairs={{0,1},{1,2},{2,3},{3,4},{4,5},{5,6},{6,7},{7,8},{8,9},{9,10},{10,1... | collective-permute-start | bytes 442376 | tf_op jit(solution)/shard_map/ppermute | solution.py:225
  295.8 203.3 %collective-permute-start.32 = (bf16[144,512]{1,0:T(8,128)(2,1)}, bf16[144,512]{1,0:T(8,128)(2,1)S(1)}, u32[]{:S(2)}, u32[]{:S(2)}) collective-permute-start(bf16[144,512]{1,0:T(8,128)(2,1)} %get-tuple-element.23), channel_id=1, source_target_pairs={{1,0},{2,1},{3,2},{4,3},{5,4},{6,5},{7,6},{8,7},{9,8},{10,9},{11,1... | collective-permute-start | bytes 442376 | tf_op jit(solution)/shard_map/ppermute | solution.py:225
  302.8 234.5 %collective-permute-start.44 = (bf16[288,512]{1,0:T(8,128)(2,1)S(1)}, bf16[288,512]{1,0:T(8,128)(2,1)S(1)}, u32[]{:S(2)}, u32[]{:S(2)}) collective-permute-start(bf16[288,512]{1,0:T(8,128)(2,1)S(1)} %shard_map.70.rest_0_), channel_id=1, source_target_pairs={{0,192},{64,128},{1,193},{65,129},{2,194},{66,130},{3,195},{67,131... | collective-permute-start | bytes 884744 | tf_op jit(solution)/shard_map/ppermute | solution.py:277
  497.2 19.4 %collective-permute-start.41 = (bf16[144,512]{1,0:T(8,128)(2,1)S(1)}, bf16[144,512]{1,0:T(8,128)(2,1)S(1)}, u32[]{:S(2)}, u32[]{:S(2)}) collective-permute-start(bf16[144,512]{1,0:T(8,128)(2,1)S(1)} %get-tuple-element.28), channel_id=1, source_target_pairs={{0,1},{1,2},{2,3},{3,4},{4,5},{5,6},{6,7},{7,8},{8,9},{9,10},{10,1... | collective-permute-start | bytes 442376 | tf_op jit(solution)/shard_map/ppermute | solution.py:225
  499.2 19.0 %collective-permute-start.42 = (bf16[144,512]{1,0:T(8,128)(2,1)S(1)}, bf16[144,512]{1,0:T(8,128)(2,1)S(1)}, u32[]{:S(2)}, u32[]{:S(2)}) collective-permute-start(bf16[144,512]{1,0:T(8,128)(2,1)S(1)} %get-tuple-element.27), channel_id=1, source_target_pairs={{1,0},{2,1},{3,2},{4,3},{5,4},{6,5},{7,6},{8,7},{9,8},{10,9},{11,1... | collective-permute-start | bytes 442376 | tf_op jit(solution)/shard_map/ppermute | solution.py:225
  516.6 74.7 %collective-permute-start.47 = (bf16[288,512]{1,0:T(8,128)(2,1)S(1)}, bf16[288,512]{1,0:T(8,128)(2,1)}, u32[]{:S(2)}, u32[]{:S(2)}) collective-permute-start(bf16[288,512]{1,0:T(8,128)(2,1)S(1)} %shard_map.70.rest_0_), channel_id=1, source_target_pairs={{64,0},{65,1},{66,2},{67,3},{68,4},{69,5},{70,6},{71,7},{72,8},{73... | collective-permute-start | bytes 884744 | tf_op jit(solution)/shard_map/ppermute | solution.py:277
  518.1 10.4 %collective-permute-start.33 = (bf16[288,512]{1,0:T(8,128)(2,1)S(1)}, bf16[288,512]{1,0:T(8,128)(2,1)S(1)}, u32[]{:S(2)}, u32[]{:S(2)}) collective-permute-start(bf16[288,512]{1,0:T(8,128)(2,1)S(1)} %shard_map.67), channel_id=1, source_target_pairs={{0,192},{64,128},{1,193},{65,129},{2,194},{66,130},{3,195},{67,131... | collective-permute-start | bytes 884744 | tf_op jit(solution)/shard_map/ppermute | solution.py:277
  527.0 57.3 %collective-permute-start.38 = (bf16[288,512]{1,0:T(8,128)(2,1)S(1)}, bf16[288,512]{1,0:T(8,128)(2,1)S(1)}, u32[]{:S(2)}, u32[]{:S(2)}) collective-permute-start(bf16[288,512]{1,0:T(8,128)(2,1)S(1)} %shard_map.67), channel_id=1, source_target_pairs={{0,64},{1,65},{2,66},{3,67},{4,68},{5,69},{6,70},{7,71},{8,72},{9,... | collective-permute-start | bytes 884744 | tf_op jit(solution)/shard_map/ppermute | solution.py:277
  528.6 14.1 %collective-permute-start.43 = (bf16[288,512]{1,0:T(8,128)(2,1)S(1)}, bf16[288,512]{1,0:T(8,128)(2,1)S(1)}, u32[]{:S(2)}, u32[]{:S(2)}) collective-permute-start(bf16[288,512]{1,0:T(8,128)(2,1)S(1)} %shard_map.71), channel_id=1, source_target_pairs={{0,192},{64,128},{1,193},{65,129},{2,194},{66,130},{3,195},{67,131... | collective-permute-start | bytes 884744 | tf_op jit(solution)/shard_map/ppermute | solution.py:277
  537.3 16.1 %collective-permute-start.35 = (bf16[144,512]{1,0:T(8,128)(2,1)S(1)}, bf16[144,512]{1,0:T(8,128)(2,1)S(1)}, u32[]{:S(2)}, u32[]{:S(2)}) collective-permute-start(bf16[144,512]{1,0:T(8,128)(2,1)S(1)} %get-tuple-element.22), channel_id=1, source_target_pairs={{0,1},{1,2},{2,3},{3,4},{4,5},{5,6},{6,7},{7,8},{8,9},{9,10},{10,1... | collective-permute-start | bytes 442376 | tf_op jit(solution)/shard_map/ppermute | solution.py:225
  542.7 12.6 %collective-permute-start.36 = (bf16[144,512]{1,0:T(8,128)(2,1)S(1)}, bf16[144,512]{1,0:T(8,128)(2,1)S(1)}, u32[]{:S(2)}, u32[]{:S(2)}) collective-permute-start(bf16[144,512]{1,0:T(8,128)(2,1)S(1)} %get-tuple-element.21), channel_id=1, source_target_pairs={{1,0},{2,1},{3,2},{4,3},{5,4},{6,5},{7,6},{8,7},{9,8},{10,9},{11,1... | collective-permute-start | bytes 442376 | tf_op jit(solution)/shard_map/ppermute | solution.py:225
  553.4 16.7 %collective-permute-start.45 = (bf16[144,512]{1,0:T(8,128)(2,1)S(1)}, bf16[144,512]{1,0:T(8,128)(2,1)S(1)}, u32[]{:S(2)}, u32[]{:S(2)}) collective-permute-start(bf16[144,512]{1,0:T(8,128)(2,1)S(1)} %get-tuple-element.26), channel_id=1, source_target_pairs={{0,1},{1,2},{2,3},{3,4},{4,5},{5,6},{6,7},{7,8},{8,9},{9,10},{10,1... | collective-permute-start | bytes 442376 | tf_op jit(solution)/shard_map/ppermute | solution.py:225
  555.3 19.4 %collective-permute-start.46 = (bf16[144,512]{1,0:T(8,128)(2,1)S(1)}, bf16[144,512]{1,0:T(8,128)(2,1)S(1)}, u32[]{:S(2)}, u32[]{:S(2)}) collective-permute-start(bf16[144,512]{1,0:T(8,128)(2,1)S(1)} %get-tuple-element.25), channel_id=1, source_target_pairs={{1,0},{2,1},{3,2},{4,3},{5,4},{6,5},{7,6},{8,7},{9,8},{10,9},{11,1... | collective-permute-start | bytes 442376 | tf_op jit(solution)/shard_map/ppermute | solution.py:225
  570.1 19.5 %collective-permute-start.39 = (bf16[288,512]{1,0:T(8,128)(2,1)S(1)}, bf16[288,512]{1,0:T(8,128)(2,1)S(1)}, u32[]{:S(2)}, u32[]{:S(2)}) collective-permute-start(bf16[288,512]{1,0:T(8,128)(2,1)S(1)} %get-tuple-element.9), channel_id=1, source_target_pairs={{192,128},{193,129},{194,130},{195,131},{196,132},{197,133},{198,1... | collective-permute-start | bytes 884744 | tf_op jit(solution)/shard_map/ppermute | solution.py:277
  574.7 16.1 %collective-permute-start.40 = (bf16[288,512]{1,0:T(8,128)(2,1)S(1)}, bf16[288,512]{1,0:T(8,128)(2,1)S(1)}, u32[]{:S(2)}, u32[]{:S(2)}) collective-permute-start(bf16[288,512]{1,0:T(8,128)(2,1)S(1)} %shard_map.69), channel_id=1, source_target_pairs={{128,192},{129,193},{130,194},{131,195},{132,196},{133,197},{134,1... | collective-permute-start | bytes 884744 | tf_op jit(solution)/shard_map/ppermute | solution.py:277
  583.6 7.7 %collective-permute-start.48 = (bf16[288,512]{1,0:T(8,128)(2,1)S(1)}, bf16[288,512]{1,0:T(8,128)(2,1)S(1)}, u32[]{:S(2)}, u32[]{:S(2)}) collective-permute-start(bf16[288,512]{1,0:T(8,128)(2,1)S(1)} %shard_map.71), channel_id=1, source_target_pairs={{0,64},{1,65},{2,66},{3,67},{4,68},{5,69},{6,70},{7,71},{8,72},{9,... | collective-permute-start | bytes 884744 | tf_op jit(solution)/shard_map/ppermute | solution.py:277
  584.3 8.8 %collective-permute-start.49 = (bf16[288,512]{1,0:T(8,128)(2,1)S(1)}, bf16[288,512]{1,0:T(8,128)(2,1)}, u32[]{:S(2)}, u32[]{:S(2)}) collective-permute-start(bf16[288,512]{1,0:T(8,128)(2,1)S(1)} %get-tuple-element.11), channel_id=1, source_target_pairs={{192,128},{193,129},{194,130},{195,131},{196,132},{197,133},{198,1... | collective-permute-start | bytes 884744 | tf_op jit(solution)/shard_map/ppermute | solution.py:277
  589.6 8.7 %collective-permute-start.50 = (bf16[288,512]{1,0:T(8,128)(2,1)S(1)}, bf16[288,512]{1,0:T(8,128)(2,1)}, u32[]{:S(2)}, u32[]{:S(2)}) collective-permute-start(bf16[288,512]{1,0:T(8,128)(2,1)S(1)} %shard_map.73), channel_id=1, source_target_pairs={{128,192},{129,193},{130,194},{131,195},{132,196},{133,197},{134,1... | collective-permute-start | bytes 884744 | tf_op jit(solution)/shard_map/ppermute | solution.py:277
  (17 other events, 197.1 us)
